TPU v7x, 256 devices: a whole 4x4x8 slice. The times are simulated.
256 devices in a mesh: context: 64 (over z, x, core), channel: 4 (over y).
Axes of the slice: x: 4, y: 4, z: 8, core: 2. Of those that a mesh axis runs over, the one named last changes fastest.
Arguments:
- inputs: bfloat16 [2048, 16384], P('channel', 'context'), may hold values from -6 to 6
- out_grad: bfloat16 [2048, 16384], P('channel', 'context'), may hold values from -6 to 6
- low_pass: float32 [2, 2048], P(None, 'channel'), may hold values from 0.75 to 1.25
- high_pass: float32 [2, 2048], P(None, 'channel'), may hold values from -3 to 3
- level_weight: float32 [12, 2048], P(None, 'channel'), may hold values from -1.75 to 1.75
- mix: bfloat16 [2048, 2048], P(None, 'channel'), may hold values from -0.125 to 0.125
Outputs:
- grad_inputs: bfloat16 [2048, 16384], P('channel', 'context')
- grad_low: float32 [2, 2048], P(None, 'channel')
- grad_high: float32 [2, 2048], P(None, 'channel')
- grad_level: float32 [12, 2048], P(None, 'channel')
- grad_mix: float32 [2048, 2048], P('context', 'channel')
All inputs are finite; a program needn't handle non-finite values.
Results may differ from a plain program's by a relative error of at most 0.012.
Values may be sent and summed in bfloat16 or wider, within the bound.
No kernel may reach another device: no remote copies, remote signals or barrier semaphores. Data moves between devices by JAX's collectives and lax.ppermute only.
A program may use at most 64 MiB of HBM per device.

v0:
```python
import jax
import jax.numpy as jnp
from jax import lax
from jax.sharding import PartitionSpec as P

HALF_ROOT = 0.5**0.5


def passed_along(value, axis, steps):
    count = lax.axis_size(axis)
    leading, last = (max(0, -steps), min(count, count - steps))
    return lax.ppermute(value, axis, [(source, source + steps) for source in range(leading, last)])


def advance(present, lagged, low_taps, high_taps):
    present_wide = present.astype(jnp.float32)
    lagged_wide = lagged.astype(jnp.float32)
    branch = HALF_ROOT * (high_taps[0] * present_wide + high_taps[1] * lagged_wide)
    present_next = (HALF_ROOT * (low_taps[0] * present_wide + low_taps[1] * lagged_wide)).astype(
        jnp.bfloat16
    )
    return (present_next, branch)


def terms_of(present, lagged, grad_now, grad_branch, grad_mixed, high_taps):
    present_wide = present.astype(jnp.float32)
    lagged_wide = lagged.astype(jnp.float32)
    branch = HALF_ROOT * (high_taps[0] * present_wide + high_taps[1] * lagged_wide)
    low_terms = HALF_ROOT * jnp.stack(
        [jnp.sum(present_wide * grad_now, 1), jnp.sum(lagged_wide * grad_now, 1)]
    )
    high_terms = HALF_ROOT * jnp.stack(
        [jnp.sum(present_wide * grad_branch, 1), jnp.sum(lagged_wide * grad_branch, 1)]
    )
    return (low_terms, high_terms, jnp.sum(grad_mixed * branch, 1))


def split_grad(grad_now, grad_branch, low_taps, high_taps):
    direct_part = HALF_ROOT * (low_taps[0] * grad_now + high_taps[0] * grad_branch)
    lagged_part = HALF_ROOT * (low_taps[1] * grad_now + high_taps[1] * grad_branch)
    return (direct_part, lagged_part)


def shards(inputs, out_grad, low_pass, high_pass, level_weight, mix):
    channels, length = inputs.shape
    levels = level_weight.shape[0] - 1
    local_count = length.bit_length() - 1
    low_taps = low_pass[:, :, None]
    high_taps = high_pass[:, :, None]
    weights = level_weight[:, :, None]
    stored = []
    mixed_sum = jnp.zeros((channels, length), jnp.float32)
    current = inputs
    for level_index in range(local_count):
        distance = 2**level_index
        edge_rows = passed_along(current[:, length - distance :], "context", 1)
        lagged = jnp.concatenate([edge_rows, current[:, : length - distance]], 1)
        stored.append((current, lagged))
        current, branch = advance(current, lagged, low_taps, high_taps)
        mixed_sum = mixed_sum + weights[level_index + 1] * branch
    for hop_index in range(levels - local_count):
        level_index = local_count + hop_index
        lagged = passed_along(current, "context", 2**hop_index)
        stored.append((current, lagged))
        current, branch = advance(current, lagged, low_taps, high_taps)
        mixed_sum = mixed_sum + weights[level_index + 1] * branch
    mixed_sum = mixed_sum + weights[0] * current.astype(jnp.float32)
    z_out = jax.nn.gelu(mixed_sum).astype(jnp.bfloat16)
    partial_mix = lax.dot_general(
        lax.all_gather(z_out, "channel", axis=0, tiled=True),
        out_grad,
        (((1,), (1,)), ((), ())),
        preferred_element_type=jnp.float32,
    )
    scale = float(lax.axis_size("context") * length) ** (-0.5)
    grad_mix = lax.psum_scatter(partial_mix, "context", scatter_dimension=0, tiled=True) * scale
    grad_z = lax.psum_scatter(
        jnp.dot(mix, out_grad, preferred_element_type=jnp.float32),
        "channel",
        scatter_dimension=0,
        tiled=True,
    )
    grad_mixed = jax.vjp(jax.nn.gelu, mixed_sum)[1](grad_z)[0]
    totals = [jnp.zeros((2, channels), jnp.float32), jnp.zeros((2, channels), jnp.float32)]
    rows_out = [None] * (levels + 1)
    first_row = jnp.sum(grad_mixed * current.astype(jnp.float32), 1)

    def record(level_index, found):
        found = lax.psum(found, "context")
        totals[0] = totals[0] + found[0]
        totals[1] = totals[1] + found[1]
        rows_out[level_index + 1] = found[2]
        if len(found) == 4:
            rows_out[0] = found[3]

    grad_now = weights[0] * grad_mixed
    for step_index in range(levels - local_count):
        level_index = levels - 1 - step_index
        hop_index = level_index - local_count
        present, lagged = stored[level_index]
        grad_branch = weights[level_index + 1] * grad_mixed
        found = terms_of(present, lagged, grad_now, grad_branch, grad_mixed, high_taps)
        if step_index == 0:
            found = found + (first_row,)
        record(level_index, found)
        direct_part, lagged_part = split_grad(grad_now, grad_branch, low_taps, high_taps)
        grad_now = direct_part + passed_along(lagged_part, "context", -(2**hop_index))
    for step_index in range(local_count):
        level_index = local_count - 1 - step_index
        distance = 2**level_index
        present, lagged = stored[level_index]
        grad_branch = weights[level_index + 1] * grad_mixed
        record(level_index, terms_of(present, lagged, grad_now, grad_branch, grad_mixed, high_taps))
        direct_part, lagged_part = split_grad(grad_now, grad_branch, low_taps, high_taps)
        edge_rows = passed_along(lagged_part[:, :distance], "context", -1)
        grad_now = direct_part + jnp.concatenate([lagged_part[:, distance:], edge_rows], 1)
    low_grad, high_grad, level_grad = (totals[0], totals[1], jnp.stack(rows_out))
    return (
        grad_now.astype(jnp.bfloat16),
        low_grad * scale,
        high_grad * scale,
        level_grad * scale,
        grad_mix,
    )


def solution(mesh):
    return jax.shard_map(
        shards,
        mesh=mesh,
        in_specs=(
            P("channel", "context"),
            P("channel", "context"),
            P(None, "channel"),
            P(None, "channel"),
            P(None, "channel"),
            P(None, "channel"),
        ),
        out_specs=(
            P("channel", "context"),
            P(None, "channel"),
            P(None, "channel"),
            P(None, "channel"),
            P("context", "channel"),
        ),
        check_vma=False,
    )
```

profile of v0, /device:TPU:152, one launch (start us, length us, event | category | flops | bytes accessed | tf_op | source)
XLA Modules:
  0.0 537.8 jit_solution(5035400398749323138)
XLA Ops:
  8.4 1.9 collective-permute-start
  11.1 6.9 %collective-permute-done = bf16[512,1]{1,0:T(8,128)(2,1)S(1)} collective-permute-done((bf16[512,1]{1,0:T(8,128)(2,1)S(1)}, bf16[512,1]{1,0:T(8,128)(2,1)S(1)}, u32[]{:S(2)}, u32[]{:S(2)}) %collective-permute-start) | collective-permute-done | bytes 1056 | tf_op jit(solution)/shard_map/ppermute | solution.py:12
  19.5 1.9 collective-permute-start.1
  21.4 7.7 %collective-permute-done.1 = bf16[512,2]{1,0:T(8,128)(2,1)S(1)} collective-permute-done((bf16[512,2]{1,0:T(8,128)(2,1)S(1)}, bf16[512,2]{1,0:T(8,128)(2,1)S(1)}, u32[]{:S(2)}, u32[]{:S(2)}) %collective-permute-start.1) | collective-permute-done | bytes 2080 | tf_op jit(solution)/shard_map/ppermute | solution.py:12
  29.5 1.9 collective-permute-start.2
  31.4 7.7 %collective-permute-done.2 = bf16[512,4]{1,0:T(8,128)(2,1)S(1)} collective-permute-done((bf16[512,4]{1,0:T(8,128)(2,1)S(1)}, bf16[512,4]{1,0:T(8,128)(2,1)S(1)}, u32[]{:S(2)}, u32[]{:S(2)}) %collective-permute-start.2) | collective-permute-done | bytes 4128 | tf_op jit(solution)/shard_map/ppermute | solution.py:12
  39.6 1.9 collective-permute-start.3
  41.5 2.0 fusion.122
  43.6 5.6 %collective-permute-done.3 = bf16[512,8]{1,0:T(8,128)(2,1)S(1)} collective-permute-done((bf16[512,8]{1,0:T(8,128)(2,1)S(1)}, bf16[512,8]{1,0:T(8,128)(2,1)S(1)}, u32[]{:S(2)}, u32[]{:S(2)}) %collective-permute-start.3) | collective-permute-done | bytes 8224 | tf_op jit(solution)/shard_map/ppermute | solution.py:12
  49.6 1.9 collective-permute-start.4
  51.5 7.7 %collective-permute-done.4 = bf16[512,16]{1,0:T(8,128)(2,1)S(1)} collective-permute-done((bf16[512,16]{1,0:T(8,128)(2,1)S(1)}, bf16[512,16]{1,0:T(8,128)(2,1)S(1)}, u32[]{:S(2)}, u32[]{:S(2)}) %collective-permute-start.4) | collective-permute-done | bytes 16416 | tf_op jit(solution)/shard_map/ppermute | solution.py:12
  59.6 1.9 collective-permute-start.5
  61.6 7.7 %collective-permute-done.5 = bf16[512,32]{1,0:T(8,128)(2,1)S(1)} collective-permute-done((bf16[512,32]{1,0:T(8,128)(2,1)S(1)}, bf16[512,32]{1,0:T(8,128)(2,1)S(1)}, u32[]{:S(2)}, u32[]{:S(2)}) %collective-permute-start.5) | collective-permute-done | bytes 32800 | tf_op jit(solution)/shard_map/ppermute | solution.py:12
  69.7 2.1 collective-permute-start.6
  71.9 7.5 %collective-permute-done.6 = bf16[512,64]{1,0:T(8,128)(2,1)S(1)} collective-permute-done((bf16[512,64]{1,0:T(8,128)(2,1)S(1)}, bf16[512,64]{1,0:T(8,128)(2,1)S(1)}, u32[]{:S(2)}, u32[]{:S(2)}) %collective-permute-start.6) | collective-permute-done | bytes 65568 | tf_op jit(solution)/shard_map/ppermute | solution.py:12
  79.8 1.9 collective-permute-start.7
  81.8 7.7 %collective-permute-done.7 = bf16[512,128]{1,0:T(8,128)(2,1)S(1)} collective-permute-done((bf16[512,128]{1,0:T(8,128)(2,1)S(1)}, bf16[512,128]{1,0:T(8,128)(2,1)S(1)}, u32[]{:S(2)}, u32[]{:S(2)}) %collective-permute-start.7) | collective-permute-done | bytes 131104 | tf_op jit(solution)/shard_map/ppermute | solution.py:12
  89.6 1.9 collective-permute-start.8
  91.6 9.0 %collective-permute-done.8 = bf16[512,256]{1,0:T(8,128)(2,1)S(1)} collective-permute-done((bf16[512,256]{1,0:T(8,128)(2,1)S(1)}, bf16[512,256]{1,0:T(8,128)(2,1)S(1)}, u32[]{:S(2)}, u32[]{:S(2)}) %collective-permute-start.8) | collective-permute-done | bytes 262176 | tf_op jit(solution)/shard_map/ppermute | solution.py:12
  102.9 11.4 %collective-permute-done.9 = bf16[512,256]{1,0:T(8,128)(2,1)S(1)} collective-permute-done((bf16[512,256]{1,0:T(8,128)(2,1)S(1)}, bf16[512,256]{1,0:T(8,128)(2,1)S(1)}, u32[]{:S(2)}, u32[]{:S(2)}) %collective-permute-start.9) | collective-permute-done | bytes 262176 | tf_op jit(solution)/shard_map/ppermute | solution.py:12
  116.4 9.9 %collective-permute-done.10 = bf16[512,256]{1,0:T(8,128)(2,1)S(1)} collective-permute-done((bf16[512,256]{1,0:T(8,128)(2,1)S(1)}, bf16[512,256]{1,0:T(8,128)(2,1)S(1)}, u32[]{:S(2)}, u32[]{:S(2)}) %collective-permute-start.10) | collective-permute-done | bytes 262176 | tf_op jit(solution)/shard_map/ppermute | solution.py:12
  127.1 3.7 multiply_convert_fusion
  130.8 2.5 add_multiply_fusion.10
  135.3 10.8 %collective-permute-done.11 = f32[512,256]{1,0:T(8,128)} collective-permute-done((f32[512,256]{1,0:T(8,128)}, f32[512,256]{1,0:T(8,128)}, u32[]{:S(2)}, u32[]{:S(2)}) %collective-permute-start.11) | collective-permute-done | bytes 524320 | tf_op jit(solution)/shard_map/ppermute | solution.py:12
  149.7 9.1 %collective-permute-done.12 = f32[512,256]{1,0:T(8,128)S(1)} collective-permute-done((f32[512,256]{1,0:T(8,128)S(1)}, f32[512,256]{1,0:T(8,128)S(1)}, u32[]{:S(2)}, u32[]{:S(2)}) %collective-permute-start.12) | collective-permute-done | bytes 524320 | tf_op jit(solution)/shard_map/ppermute | solution.py:12
  158.8 3.7 multiply_reduce_fusion
  166.4 4.0 fusion.123
  170.5 2.9 collective-permute-done.13
  173.4 3.5 fusion.68
  177.2 7.1 %collective-permute-start.14 = (f32[512,128]{1,0:T(8,128)S(1)}, f32[512,128]{1,0:T(8,128)S(1)}, u32[]{:S(2)}, u32[]{:S(2)}) collective-permute-start(f32[512,128]{1,0:T(8,128)S(1)} %get-tuple-element.137), channel_id=1, source_target_pairs={{4,0},{8,4},{12,8},{16,12},{20,16},{24,20},{28,24},{32,28},{36,32}... | collective-permute-start | bytes 786440 | tf_op jit(solution)/shard_map/ppermute | solution.py:12
  184.4 3.9 collective-permute-done.14
  189.2 7.3 %collective-permute-start.15 = (f32[512,64]{1,0:T(8,128)S(1)}, f32[512,64]{1,0:T(8,128)S(1)}, u32[]{:S(2)}, u32[]{:S(2)}) collective-permute-start(f32[512,64]{1,0:T(8,128)S(1)} %slice.343), channel_id=1, source_target_pairs={{4,0},{8,4},{12,8},{16,12},{20,16},{24,20},{28,24},{32,28},{36,32}... | collective-permute-start | bytes 393224 | tf_op jit(solution)/shard_map/ppermute | solution.py:12
  196.7 3.5 collective-permute-done.15
  200.2 2.6 fusion.52
  203.1 7.1 %collective-permute-start.16 = (f32[512,32]{1,0:T(8,128)S(1)}, f32[512,32]{1,0:T(8,128)S(1)}, u32[]{:S(2)}, u32[]{:S(2)}) collective-permute-start(f32[512,32]{1,0:T(8,128)S(1)} %slice.345), channel_id=1, source_target_pairs={{4,0},{8,4},{12,8},{16,12},{20,16},{24,20},{28,24},{32,28},{36,32}... | collective-permute-start | bytes 196616 | tf_op jit(solution)/shard_map/ppermute | solution.py:12
  210.4 3.7 collective-permute-done.16
  215.1 7.1 %collective-permute-start.17 = (f32[512,16]{1,0:T(8,128)S(1)}, f32[512,16]{1,0:T(8,128)S(1)}, u32[]{:S(2)}, u32[]{:S(2)}) collective-permute-start(f32[512,16]{1,0:T(8,128)S(1)} %slice.347), channel_id=1, source_target_pairs={{4,0},{8,4},{12,8},{16,12},{20,16},{24,20},{28,24},{32,28},{36,32}... | collective-permute-start | bytes 98312 | tf_op jit(solution)/shard_map/ppermute | solution.py:12
  222.5 3.7 collective-permute-done.17
  226.2 2.6 fusion.36
  229.0 7.1 %collective-permute-start.18 = (f32[512,8]{1,0:T(8,128)S(1)}, f32[512,8]{1,0:T(8,128)S(1)}, u32[]{:S(2)}, u32[]{:S(2)}) collective-permute-start(f32[512,8]{1,0:T(8,128)S(1)} %slice.349), channel_id=1, source_target_pairs={{4,0},{8,4},{12,8},{16,12},{20,16},{24,20},{28,24},{32,28},{36,32}... | collective-permute-start | bytes 49160 | tf_op jit(solution)/shard_map/ppermute | solution.py:12
  236.4 3.7 collective-permute-done.18
  241.1 7.1 %collective-permute-start.19 = (f32[512,4]{1,0:T(8,128)S(1)}, f32[512,4]{1,0:T(8,128)S(1)}, u32[]{:S(2)}, u32[]{:S(2)}) collective-permute-start(f32[512,4]{1,0:T(8,128)S(1)} %slice.351), channel_id=1, source_target_pairs={{4,0},{8,4},{12,8},{16,12},{20,16},{24,20},{28,24},{32,28},{36,32}... | collective-permute-start | bytes 24584 | tf_op jit(solution)/shard_map/ppermute | solution.py:12
  248.5 3.8 collective-permute-done.19
  252.3 2.6 fusion.20
  255.2 7.2 %collective-permute-start.20 = (f32[512,2]{1,0:T(8,128)S(1)}, f32[512,2]{1,0:T(8,128)S(1)}, u32[]{:S(2)}, u32[]{:S(2)}) collective-permute-start(f32[512,2]{1,0:T(8,128)S(1)} %slice.353), channel_id=1, source_target_pairs={{4,0},{8,4},{12,8},{16,12},{20,16},{24,20},{28,24},{32,28},{36,32}... | collective-permute-start | bytes 12296 | tf_op jit(solution)/shard_map/ppermute | solution.py:12
  263.3 5.0 collective-permute-done.20
  270.7 7.1 %collective-permute-start.21 = (f32[512,1]{1,0:T(8,128)}, f32[512,1]{1,0:T(8,128)S(1)}, u32[]{:S(2)}, u32[]{:S(2)}) collective-permute-start(f32[512,1]{1,0:T(8,128)} %slice.355), channel_id=1, source_target_pairs={{4,0},{8,4},{12,8},{16,12},{20,16},{24,20},{28,24},{32,28},{36,32}... | collective-permute-start | bytes 6152 | tf_op jit(solution)/shard_map/ppermute | solution.py:12
  278.0 247.6 %all-reduce = (f32[2,512]{1,0:T(2,128)S(1)}, f32[2,512]{1,0:T(2,128)S(1)}, f32[1,512]{1,0:T(1,128)S(1)}, f32[1,512]{1,0:T(1,128)S(1)}, f32[1,512]{1,0:T(1,128)S(...) all-reduce(f32[2,512]{1,0:T(2,128)S(1)} %fusion.114, ...), channel_id=1, replica_groups=mesh['context'=64,'channel'=4] {'context'}, use_global_device_ids=true, to_apply=%region_3.0 | all-reduce | flops 8192 | bytes 65536 | tf_op jit(solution)/shard_map/psum | solution.py:89
  (237 shorter events, 34.4 us)
Async XLA Ops:
  7.2 34.3 %copy-start = (bf16[2048,512]{1,0:T(8,128)(2,1)S(1)}, bf16[2048,512]{1,0:T(8,128)(2,1)}, u32[]{:S(2)}) copy-start(bf16[2048,512]{1,0:T(8,128)(2,1)} %param.11) | copy-start | bytes 6291460
  7.2 123.6 %reduce-scatter.3.cloned.1.call-start = ((), (), s32[]{:S(2)}) async-start(), calls=%async_computation.2 | async-start | bytes 2621440 | tf_op jit(solution)/shard_map/reduce_scatter | solution.py:77
  7.2 34.3 %copy-start.42 = (bf16[512,256]{1,0:T(8,128)(2,1)S(1)}, bf16[512,256]{1,0:T(8,128)(2,1)}, u32[]{:S(2)}) copy-start(bf16[512,256]{1,0:T(8,128)(2,1)} %param.7) | copy-start | bytes 786436
  8.4 9.6 %collective-permute-start = (bf16[512,1]{1,0:T(8,128)(2,1)S(1)}, bf16[512,1]{1,0:T(8,128)(2,1)S(1)}, u32[]{:S(2)}, u32[]{:S(2)}) collective-permute-start(bf16[512,1]{1,0:T(8,128)(2,1)S(1)} %slice.116), channel_id=1, source_target_pairs={{0,4},{4,8},{8,12},{12,16},{16,20},{20,24},{24,28},{28,32},{32,36}... | collective-permute-start | bytes 3080 | tf_op jit(solution)/shard_map/ppermute | solution.py:12
  19.4 107.0 %copy-start.3 = (bf16[512,256]{1,0:T(8,128)(2,1)}, bf16[512,256]{1,0:T(8,128)(2,1)S(1)}, u32[]{:S(2)}) copy-start(bf16[512,256]{1,0:T(8,128)(2,1)S(1)} %fusion.11) | copy-start | bytes 786436
  19.5 9.6 %collective-permute-start.1 = (bf16[512,2]{1,0:T(8,128)(2,1)S(1)}, bf16[512,2]{1,0:T(8,128)(2,1)S(1)}, u32[]{:S(2)}, u32[]{:S(2)}) collective-permute-start(bf16[512,2]{1,0:T(8,128)(2,1)S(1)} %slice.160), channel_id=1, source_target_pairs={{0,4},{4,8},{8,12},{12,16},{16,20},{20,24},{24,28},{28,32},{32,36}... | collective-permute-start | bytes 6152 | tf_op jit(solution)/shard_map/ppermute | solution.py:12
  29.5 9.6 %collective-permute-start.2 = (bf16[512,4]{1,0:T(8,128)(2,1)S(1)}, bf16[512,4]{1,0:T(8,128)(2,1)S(1)}, u32[]{:S(2)}, u32[]{:S(2)}) collective-permute-start(bf16[512,4]{1,0:T(8,128)(2,1)S(1)} %slice.162), channel_id=1, source_target_pairs={{0,4},{4,8},{8,12},{12,16},{16,20},{20,24},{24,28},{28,32},{32,36}... | collective-permute-start | bytes 12296 | tf_op jit(solution)/shard_map/ppermute | solution.py:12
  39.6 9.6 %collective-permute-start.3 = (bf16[512,8]{1,0:T(8,128)(2,1)S(1)}, bf16[512,8]{1,0:T(8,128)(2,1)S(1)}, u32[]{:S(2)}, u32[]{:S(2)}) collective-permute-start(bf16[512,8]{1,0:T(8,128)(2,1)S(1)} %slice.164), channel_id=1, source_target_pairs={{0,4},{4,8},{8,12},{12,16},{16,20},{20,24},{24,28},{28,32},{32,36}... | collective-permute-start | bytes 24584 | tf_op jit(solution)/shard_map/ppermute | solution.py:12
  43.5 122.8 %all-gather.2.cloned.1.call-start = ((), (), s32[]{:S(2)}) async-start(), calls=%async_computation.3 | async-start | bytes 1310720 | tf_op jit(solution)/shard_map/all_gather | solution.py:70
  49.5 32.3 %copy-start.78 = (f32[2,512]{1,0:T(2,128)S(1)}, f32[2,512]{1,0:T(2,128)}, u32[]{:S(2)}) copy-start(f32[2,512]{1,0:T(2,128)} %param.9) | copy-start | bytes 12292
  49.6 9.6 %collective-permute-start.4 = (bf16[512,16]{1,0:T(8,128)(2,1)S(1)}, bf16[512,16]{1,0:T(8,128)(2,1)S(1)}, u32[]{:S(2)}, u32[]{:S(2)}) collective-permute-start(bf16[512,16]{1,0:T(8,128)(2,1)S(1)} %slice.332), channel_id=1, source_target_pairs={{0,4},{4,8},{8,12},{12,16},{16,20},{20,24},{24,28},{28,32},{32,36}... | collective-permute-start | bytes 49160 | tf_op jit(solution)/shard_map/ppermute | solution.py:12
  59.2 67.2 %copy-start.26 = (bf16[512,16]{1,0:T(8,128)(2,1)}, bf16[512,16]{1,0:T(8,128)(2,1)S(1)}, u32[]{:S(2)}) copy-start(bf16[512,16]{1,0:T(8,128)(2,1)S(1)} %collective-permute-done.4) | copy-start | bytes 49156
  59.5 66.9 %copy-start.8 = (bf16[512,256]{1,0:T(8,128)(2,1)}, bf16[512,256]{1,0:T(8,128)(2,1)S(1)}, u32[]{:S(2)}) copy-start(bf16[512,256]{1,0:T(8,128)(2,1)S(1)} %fusion.43) | copy-start | bytes 786436
  59.6 9.6 %collective-permute-start.5 = (bf16[512,32]{1,0:T(8,128)(2,1)S(1)}, bf16[512,32]{1,0:T(8,128)(2,1)S(1)}, u32[]{:S(2)}, u32[]{:S(2)}) collective-permute-start(bf16[512,32]{1,0:T(8,128)(2,1)S(1)} %slice.334), channel_id=1, source_target_pairs={{0,4},{4,8},{8,12},{12,16},{16,20},{20,24},{24,28},{28,32},{32,36}... | collective-permute-start | bytes 98312 | tf_op jit(solution)/shard_map/ppermute | solution.py:12
  69.2 57.2 %copy-start.37 = (bf16[512,32]{1,0:T(8,128)(2,1)}, bf16[512,32]{1,0:T(8,128)(2,1)S(1)}, u32[]{:S(2)}) copy-start(bf16[512,32]{1,0:T(8,128)(2,1)S(1)} %collective-permute-done.5) | copy-start | bytes 98308
  69.5 57.5 %copy-start.1 = (bf16[512,256]{1,0:T(8,128)(2,1)S(1)}, bf16[512,256]{1,0:T(8,128)(2,1)}, u32[]{:S(2)}) copy-start(bf16[512,256]{1,0:T(8,128)(2,1)} %param.6) | copy-start | bytes 786436
  69.6 57.5 %copy-start.6 = (bf16[512,256]{1,0:T(8,128)(2,1)S(1)}, bf16[512,256]{1,0:T(8,128)(2,1)}, u32[]{:S(2)}) copy-start(bf16[512,256]{1,0:T(8,128)(2,1)} %copy-done.5) | copy-start | bytes 786436
  69.6 57.5 %copy-start.24 = (bf16[512,4]{1,0:T(8,128)(2,1)S(1)}, bf16[512,4]{1,0:T(8,128)(2,1)}, u32[]{:S(2)}) copy-start(bf16[512,4]{1,0:T(8,128)(2,1)} %copy-done.23) | copy-start | bytes 12292
  69.6 57.5 %copy-start.32 = (bf16[512,2]{1,0:T(8,128)(2,1)S(1)}, bf16[512,2]{1,0:T(8,128)(2,1)}, u32[]{:S(2)}) copy-start(bf16[512,2]{1,0:T(8,128)(2,1)} %copy-done.31) | copy-start | bytes 6148
  69.6 57.5 %copy-start.35 = (bf16[512,8]{1,0:T(8,128)(2,1)S(1)}, bf16[512,8]{1,0:T(8,128)(2,1)}, u32[]{:S(2)}) copy-start(bf16[512,8]{1,0:T(8,128)(2,1)} %copy-done.34) | copy-start | bytes 24580
  69.7 9.7 %collective-permute-start.6 = (bf16[512,64]{1,0:T(8,128)(2,1)S(1)}, bf16[512,64]{1,0:T(8,128)(2,1)S(1)}, u32[]{:S(2)}, u32[]{:S(2)}) collective-permute-start(bf16[512,64]{1,0:T(8,128)(2,1)S(1)} %slice.336), channel_id=1, source_target_pairs={{0,4},{4,8},{8,12},{12,16},{16,20},{20,24},{24,28},{28,32},{32,36}... | collective-permute-start | bytes 196616 | tf_op jit(solution)/shard_map/ppermute | solution.py:12
  71.8 31.0 %copy-start.50 = (f32[1,512]{1,0:T(1,128)}, f32[1,512]{1,0:T(1,128)S(1)}, u32[]{:S(2)}) copy-start(f32[1,512]{1,0:T(1,128)S(1)} %get-tuple-element.148) | copy-start | bytes 6148
  71.9 54.5 %copy-start.46 = (f32[1,512]{1,0:T(1,128)}, f32[1,512]{1,0:T(1,128)S(1)}, u32[]{:S(2)}) copy-start(f32[1,512]{1,0:T(1,128)S(1)} %get-tuple-element.150) | copy-start | bytes 6148
  71.9 54.5 %copy-start.47 = (f32[1,512]{1,0:T(1,128)}, f32[1,512]{1,0:T(1,128)S(1)}, u32[]{:S(2)}) copy-start(f32[1,512]{1,0:T(1,128)S(1)} %get-tuple-element.140) | copy-start | bytes 6148
  71.9 54.5 %copy-start.64 = (f32[1,512]{1,0:T(1,128)}, f32[1,512]{1,0:T(1,128)S(1)}, u32[]{:S(2)}) copy-start(f32[1,512]{1,0:T(1,128)S(1)} %get-tuple-element.151) | copy-start | bytes 6148
  71.9 54.5 %copy-start.45 = (f32[1,512]{1,0:T(1,128)}, f32[1,512]{1,0:T(1,128)S(1)}, u32[]{:S(2)}) copy-start(f32[1,512]{1,0:T(1,128)S(1)} %get-tuple-element.149) | copy-start | bytes 6148
  79.4 47.0 %copy-start.28 = (bf16[512,64]{1,0:T(8,128)(2,1)}, bf16[512,64]{1,0:T(8,128)(2,1)S(1)}, u32[]{:S(2)}) copy-start(bf16[512,64]{1,0:T(8,128)(2,1)S(1)} %collective-permute-done.6) | copy-start | bytes 196612
  79.8 46.7 %copy-start.10 = (bf16[512,256]{1,0:T(8,128)(2,1)}, bf16[512,256]{1,0:T(8,128)(2,1)S(1)}, u32[]{:S(2)}) copy-start(bf16[512,256]{1,0:T(8,128)(2,1)S(1)} %fusion.59) | copy-start | bytes 786436
  79.8 46.7 %copy-start.30 = (bf16[512,128]{1,0:T(8,128)(2,1)}, bf16[512,128]{1,0:T(8,128)(2,1)S(1)}, u32[]{:S(2)}) copy-start(bf16[512,128]{1,0:T(8,128)(2,1)S(1)} %get-tuple-element.139) | copy-start | bytes 393220
  79.8 9.6 %collective-permute-start.7 = (bf16[512,128]{1,0:T(8,128)(2,1)S(1)}, bf16[512,128]{1,0:T(8,128)(2,1)S(1)}, u32[]{:S(2)}, u32[]{:S(2)}) collective-permute-start(bf16[512,128]{1,0:T(8,128)(2,1)S(1)} %get-tuple-element.138), channel_id=1, source_target_pairs={{0,4},{4,8},{8,12},{12,16},{16,20},{20,24},{24,28},{28,32},{32,36}... | collective-permute-start | bytes 393224 | tf_op jit(solution)/shard_map/ppermute | solution.py:12
  89.4 37.0 %copy-start.39 = (bf16[512,128]{1,0:T(8,128)(2,1)}, bf16[512,128]{1,0:T(8,128)(2,1)S(1)}, u32[]{:S(2)}) copy-start(bf16[512,128]{1,0:T(8,128)(2,1)S(1)} %collective-permute-done.7) | copy-start | bytes 393220
  89.6 36.8 %copy-start.12 = (bf16[512,256]{1,0:T(8,128)(2,1)}, bf16[512,256]{1,0:T(8,128)(2,1)S(1)}, u32[]{:S(2)}) copy-start(bf16[512,256]{1,0:T(8,128)(2,1)S(1)} %fusion.67) | copy-start | bytes 786436
  89.6 11.0 %collective-permute-start.8 = (bf16[512,256]{1,0:T(8,128)(2,1)S(1)}, bf16[512,256]{1,0:T(8,128)(2,1)S(1)}, u32[]{:S(2)}, u32[]{:S(2)}) collective-permute-start(bf16[512,256]{1,0:T(8,128)(2,1)S(1)} %fusion.67), channel_id=1, source_target_pairs={{0,4},{4,8},{8,12},{12,16},{16,20},{20,24},{24,28},{28,32},{32,36}... | collective-permute-start | bytes 786440 | tf_op jit(solution)/shard_map/ppermute | solution.py:12
  100.9 13.4 %collective-permute-start.9 = (bf16[512,256]{1,0:T(8,128)(2,1)S(1)}, bf16[512,256]{1,0:T(8,128)(2,1)S(1)}, u32[]{:S(2)}, u32[]{:S(2)}) collective-permute-start(bf16[512,256]{1,0:T(8,128)(2,1)S(1)} %fusion.75), channel_id=1, source_target_pairs={{0,8},{4,12},{8,16},{12,20},{16,24},{20,28},{24,32},{28,36},{32,40... | collective-permute-start | bytes 786440 | tf_op jit(solution)/shard_map/ppermute | solution.py:12
  114.5 11.9 %collective-permute-start.10 = (bf16[512,256]{1,0:T(8,128)(2,1)S(1)}, bf16[512,256]{1,0:T(8,128)(2,1)S(1)}, u32[]{:S(2)}, u32[]{:S(2)}) collective-permute-start(bf16[512,256]{1,0:T(8,128)(2,1)S(1)} %fusion.83), channel_id=1, source_target_pairs={{0,16},{4,20},{8,24},{12,28},{16,32},{20,36},{24,40},{28,44},{32,4... | collective-permute-start | bytes 786440 | tf_op jit(solution)/shard_map/ppermute | solution.py:12
  133.2 12.9 %collective-permute-start.11 = (f32[512,256]{1,0:T(8,128)}, f32[512,256]{1,0:T(8,128)}, u32[]{:S(2)}, u32[]{:S(2)}) collective-permute-start(f32[512,256]{1,0:T(8,128)} %get-tuple-element.134), channel_id=1, source_target_pairs={{16,0},{20,4},{24,8},{28,12},{32,16},{36,20},{40,24},{44,28},{48,3... | collective-permute-start | bytes 1572872 | tf_op jit(solution)/shard_map/ppermute | solution.py:12
  135.2 394.6 %reduce-scatter.5.cloned.1.call-start = ((), (), s32[]{:S(2)}) async-start(), calls=%async_computation.4 | async-start | bytes 4259840 | tf_op jit(solution)/shard_map/reduce_scatter | solution.py:76
  147.7 11.1 %collective-permute-start.12 = (f32[512,256]{1,0:T(8,128)S(1)}, f32[512,256]{1,0:T(8,128)S(1)}, u32[]{:S(2)}, u32[]{:S(2)}) collective-permute-start(f32[512,256]{1,0:T(8,128)S(1)} %get-tuple-element.132), channel_id=1, source_target_pairs={{8,0},{12,4},{16,8},{20,12},{24,16},{28,20},{32,24},{36,28},{40,32... | collective-permute-start | bytes 1572872 | tf_op jit(solution)/shard_map/ppermute | solution.py:12
  164.4 8.9 %collective-permute-start.13 = (f32[512,256]{1,0:T(8,128)}, f32[512,256]{1,0:T(8,128)}, u32[]{:S(2)}, u32[]{:S(2)}) collective-permute-start(f32[512,256]{1,0:T(8,128)} %add_multiply_fusion.8), channel_id=1, source_target_pairs={{4,0},{8,4},{12,8},{16,12},{20,16},{24,20},{28,24},{32,28},{36,32}... | collective-permute-start | bytes 1572872 | tf_op jit(solution)/shard_map/ppermute | solution.py:12
  177.2 11.0 %collective-permute-start.14 = (f32[512,128]{1,0:T(8,128)S(1)}, f32[512,128]{1,0:T(8,128)S(1)}, u32[]{:S(2)}, u32[]{:S(2)}) collective-permute-start(f32[512,128]{1,0:T(8,128)S(1)} %get-tuple-element.137), channel_id=1, source_target_pairs={{4,0},{8,4},{12,8},{16,12},{20,16},{24,20},{28,24},{32,28},{36,32}... | collective-permute-start | bytes 786440 | tf_op jit(solution)/shard_map/ppermute | solution.py:12
  189.2 11.0 %collective-permute-start.15 = (f32[512,64]{1,0:T(8,128)S(1)}, f32[512,64]{1,0:T(8,128)S(1)}, u32[]{:S(2)}, u32[]{:S(2)}) collective-permute-start(f32[512,64]{1,0:T(8,128)S(1)} %slice.343), channel_id=1, source_target_pairs={{4,0},{8,4},{12,8},{16,12},{20,16},{24,20},{28,24},{32,28},{36,32}... | collective-permute-start | bytes 393224 | tf_op jit(solution)/shard_map/ppermute | solution.py:12
  203.1 11.0 %collective-permute-start.16 = (f32[512,32]{1,0:T(8,128)S(1)}, f32[512,32]{1,0:T(8,128)S(1)}, u32[]{:S(2)}, u32[]{:S(2)}) collective-permute-start(f32[512,32]{1,0:T(8,128)S(1)} %slice.345), channel_id=1, source_target_pairs={{4,0},{8,4},{12,8},{16,12},{20,16},{24,20},{28,24},{32,28},{36,32}... | collective-permute-start | bytes 196616 | tf_op jit(solution)/shard_map/ppermute | solution.py:12
  215.1 11.0 %collective-permute-start.17 = (f32[512,16]{1,0:T(8,128)S(1)}, f32[512,16]{1,0:T(8,128)S(1)}, u32[]{:S(2)}, u32[]{:S(2)}) collective-permute-start(f32[512,16]{1,0:T(8,128)S(1)} %slice.347), channel_id=1, source_target_pairs={{4,0},{8,4},{12,8},{16,12},{20,16},{24,20},{28,24},{32,28},{36,32}... | collective-permute-start | bytes 98312 | tf_op jit(solution)/shard_map/ppermute | solution.py:12
  229.0 11.0 %collective-permute-start.18 = (f32[512,8]{1,0:T(8,128)S(1)}, f32[512,8]{1,0:T(8,128)S(1)}, u32[]{:S(2)}, u32[]{:S(2)}) collective-permute-start(f32[512,8]{1,0:T(8,128)S(1)} %slice.349), channel_id=1, source_target_pairs={{4,0},{8,4},{12,8},{16,12},{20,16},{24,20},{28,24},{32,28},{36,32}... | collective-permute-start | bytes 49160 | tf_op jit(solution)/shard_map/ppermute | solution.py:12
  241.1 11.2 %collective-permute-start.19 = (f32[512,4]{1,0:T(8,128)S(1)}, f32[512,4]{1,0:T(8,128)S(1)}, u32[]{:S(2)}, u32[]{:S(2)}) collective-permute-start(f32[512,4]{1,0:T(8,128)S(1)} %slice.351), channel_id=1, source_target_pairs={{4,0},{8,4},{12,8},{16,12},{20,16},{24,20},{28,24},{32,28},{36,32}... | collective-permute-start | bytes 24584 | tf_op jit(solution)/shard_map/ppermute | solution.py:12
  255.2 13.1 %collective-permute-start.20 = (f32[512,2]{1,0:T(8,128)S(1)}, f32[512,2]{1,0:T(8,128)S(1)}, u32[]{:S(2)}, u32[]{:S(2)}) collective-permute-start(f32[512,2]{1,0:T(8,128)S(1)} %slice.353), channel_id=1, source_target_pairs={{4,0},{8,4},{12,8},{16,12},{20,16},{24,20},{28,24},{32,28},{36,32}... | collective-permute-start | bytes 12296 | tf_op jit(solution)/shard_map/ppermute | solution.py:12
  268.9 259.8 %copy-start.49 = (f32[1,512]{1,0:T(1,128)S(1)}, f32[1,512]{1,0:T(1,128)}, u32[]{:S(2)}) copy-start(f32[1,512]{1,0:T(1,128)} %copy-done.47) | copy-start | bytes 6148
  270.7 258.0 %collective-permute-start.21 = (f32[512,1]{1,0:T(8,128)}, f32[512,1]{1,0:T(8,128)S(1)}, u32[]{:S(2)}, u32[]{:S(2)}) collective-permute-start(f32[512,1]{1,0:T(8,128)} %slice.355), channel_id=1, source_target_pairs={{4,0},{8,4},{12,8},{16,12},{20,16},{24,20},{28,24},{32,28},{36,32}... | collective-permute-start | bytes 6152 | tf_op jit(solution)/shard_map/ppermute | solution.py:12
  (56 other events, 885.4 us)
Sparse Core Ops, SparseCore 0:
  43.7 31.5 reduce-scatter.2
  135.3 27.2 all-gather.1
  170.6 142.2 reduce-scatter.4
where the time goes:
time: 539 us; the launch traced here: 538 us
  blocking collectives  248 us (46%)
  waiting for transfers between devices  139 us (26%)
  starting transfers between devices  84.5 us (16%)
  other arithmetic  37.3 us (7%)
  between operations  15.2 us (3%)
  local copies, waits for them, and re-layouts  8.39 us (2%)
  matrix products  6.04 us (1%)
    psum x1, blocking collectives, record(): found = lax.psum(found, 'context')  248 us
    ppermute x22, waiting for transfers between devices, passed_along(): lax.ppermute(value, axis, [(source, source + steps) for source in range(l...  139 us
    ppermute x22, starting transfers between devices, passed_along(): lax.ppermute(value, axis, [(source, source + steps) for source in range(l...  84.3 us
    reduce_sum x8, other arithmetic, terms_of(): jnp.sum(present_wide * grad_now, 1)  13.7 us
  transfers between devices with their start and end apart: 25, of which 21 were waited for; matrix products, arithmetic and copies ran while one was open for 8% of the time, Pallas kernels for 0%

commit v1 on v0

v1 whole, which is shorter than its diff:
```python
import jax
import jax.numpy as jnp
from jax import lax
from jax.experimental import pallas as pl
from jax.experimental.pallas import tpu as pltpu
from jax.sharding import Mesh
from jax.sharding import PartitionSpec as P

R = 0.5**0.5
LEVELS = 11
CTX = ("z", "x", "core")
PLANE = ("x", "core")
NZ, NX, NC, NY = 8, 4, 2, 4
ROWS = 16
SPAN = 2048
STEP = 512
BLOCK = 256
ORDER = (0, 1, 3, 2)
F32, BF16 = jnp.float32, jnp.bfloat16
L0, L1, HP, HL, W0, H0, H1, WB = 0, 1, 2, 13, 24, 25, 26, 27
PARAMS = pltpu.CompilerParams(vmem_limit_bytes=12 * 1024 * 1024)


def shift(value, axis, steps, wrap=True):
    count = {"z": NZ, "x": NX, "core": NC, "y": NY}[axis]
    pairs = [(s, (s + steps) % count) for s in range(count) if wrap or 0 <= s + steps < count]
    return lax.ppermute(value, axis, pairs)


def forward_kernel(own_ref, halo_ref, coef_ref, z_ref, slope_ref, levels_ref, level, mixed):
    for block in range(8):
        columns = pl.ds(block * BLOCK, BLOCK)
        level[:, columns] = halo_ref[block].astype(F32)
        level[:, pl.ds(SPAN + block * BLOCK, BLOCK)] = own_ref[block].astype(F32)

    def column(index):
        return coef_ref[:, index : index + 1]

    for j in range(LEVELS):
        d = 2**j
        low0, low1 = column(L0), column(L1)
        high0, high1 = column(HP + j), column(HL + j)
        for chunk in reversed(range(2 * SPAN // STEP)):
            start = chunk * STEP
            if start + STEP <= 2 * d:
                continue
            present = level[:, pl.ds(start, STEP)]
            if d >= 128:
                if start >= d:
                    lagged = level[:, pl.ds(start - d, STEP)]
                else:
                    lagged = jnp.concatenate(
                        [level[:, pl.ds(start, d - start)], level[:, pl.ds(0, STEP - d + start)]], 1
                    ) if d - start < STEP else present
            elif start == 0:
                lagged = pltpu.roll(present, d, 1)
            else:
                lagged = pltpu.roll(level[:, pl.ds(start - 128, STEP + 128)], d, 1)[:, 128:]
            after = low0 * present + low1 * lagged
            if start >= SPAN:
                columns = pl.ds(start - SPAN, STEP)
                part = high0 * present + high1 * lagged
                if j > 0:
                    part = part + mixed[:, columns]
                if j == LEVELS - 1:
                    part = part + column(W0) * after
                    cube = part * part
                    inner = 0.7978845608028654 * part * (1.0 + 0.044715 * cube)
                    curve = jnp.tanh(inner)
                    cdf = 0.5 * (1.0 + curve)
                    slope = cdf + part * (0.5 * 0.7978845608028654) * (1.0 - curve * curve) * (
                        1.0 + 3 * 0.044715 * cube
                    )
                    z = (part * cdf).astype(BF16)
                    for piece in range(STEP // BLOCK):
                        block = (start - SPAN) // BLOCK + piece
                        inside = slice(piece * BLOCK, (piece + 1) * BLOCK)
                        z_ref[block] = z[:, inside]
                        slope_ref[block] = slope[:, inside]
                else:
                    mixed[:, columns] = part
                    stored = after.astype(BF16)
                    for piece in range(STEP // BLOCK):
                        block = (start - SPAN) // BLOCK + piece
                        inside = slice(piece * BLOCK, (piece + 1) * BLOCK)
                        levels_ref[j, block] = stored[:, inside]
            if j < LEVELS - 1:
                level[:, pl.ds(start, STEP)] = after


def forward(own, halo, coef):
    rows = pl.BlockSpec((8, ROWS, BLOCK), lambda g: (0, g, 0))
    return pl.pallas_call(
        forward_kernel,
        grid=(64 // ROWS,),
        in_specs=[rows, rows, pl.BlockSpec((ROWS, 128), lambda g: (g, 0))],
        out_specs=[rows, rows, pl.BlockSpec((LEVELS - 1, 8, ROWS, BLOCK), lambda g: (0, 0, g, 0))],
        out_shape=[
            jax.ShapeDtypeStruct((8, 64, BLOCK), BF16),
            jax.ShapeDtypeStruct((8, 64, BLOCK), F32),
            jax.ShapeDtypeStruct((LEVELS - 1, 8, 64, BLOCK), BF16),
        ],
        scratch_shapes=[pltpu.VMEM((ROWS, 2 * SPAN), F32), pltpu.VMEM((ROWS, SPAN), F32)],
        compiler_params=PARAMS,
        cost_estimate=pl.CostEstimate(flops=40_000_000, bytes_accessed=4_000_000, transcendentals=131072),
        name="forward_chain",
    )(own, halo, coef)


def backward_kernel(own_ref, halo_ref, inputs_ref, levels_ref, coef_ref, out_ref, grad, mixed, small):
    group = pl.program_id(0)
    channels = pl.ds(pl.multiple_of(group * ROWS, ROWS), ROWS)

    def column(index):
        return coef_ref[:, index : index + 1]

    weight0 = column(W0)
    for block in range(8):
        for ref, at in ((own_ref, 0), (halo_ref, SPAN)):
            columns = pl.ds(at + block * BLOCK, BLOCK)
            value = ref[block].astype(F32)
            mixed[:, columns] = value
            grad[:, columns] = weight0 * value

    lanes = (ROWS, 128)

    def folded(value):
        total = value[:, :128]
        for at in range(128, value.shape[1], 128):
            total = total + value[:, at : at + 128]
        return total

    low_sums = [jnp.zeros(lanes, F32), jnp.zeros(lanes, F32)]
    high_sums = [jnp.zeros(lanes, F32), jnp.zeros(lanes, F32)]
    level_sums = [None] * (LEVELS + 1)
    for j in reversed(range(LEVELS)):
        d = 2**j
        low0, low1 = column(L0), column(L1)
        high0, high1 = column(HP + j), column(HL + j)
        weight = column(WB + j)
        gm_now = jnp.zeros(lanes, F32)
        gm_lag = jnp.zeros(lanes, F32)
        need = SPAN + (d if j else 0)
        need = -(-need // 128) * 128
        for start in range(0, need, STEP):
            size = min(STEP, need - start)
            window = pl.ds(start, size)
            g, m = grad[:, window], mixed[:, window]
            if d >= 128:
                g_next, m_next = grad[:, pl.ds(start + d, size)], mixed[:, pl.ds(start + d, size)]
            else:
                wide = pl.ds(start, size + 128)
                g_next = pltpu.roll(grad[:, wide], size + 128 - d, 1)[:, :size]
                m_next = pltpu.roll(mixed[:, wide], size + 128 - d, 1)[:, :size]
            if start < SPAN:
                pieces = []
                for piece in range(STEP // BLOCK):
                    block = start // BLOCK + piece
                    pieces.append(inputs_ref[block] if j == 0 else levels_ref[j - 1, block])
                value = jnp.concatenate(pieces, 1).astype(F32)
                low_sums[0] = low_sums[0] + folded(value * g)
                low_sums[1] = low_sums[1] + folded(value * g_next)
                gm_now = gm_now + folded(value * m)
                gm_lag = gm_lag + folded(value * m_next)
            after = low0 * g + high0 * m + low1 * g_next + high1 * m_next
            if j == 0:
                after = after.astype(BF16)
                for piece in range(STEP // BLOCK):
                    block = start // BLOCK + piece
                    out_ref[block, channels] = after[:, piece * BLOCK : (piece + 1) * BLOCK]
            else:
                grad[:, window] = after
        high_sums[0] = high_sums[0] + weight * gm_now
        high_sums[1] = high_sums[1] + weight * gm_lag
        level_sums[j + 1] = column(H0) * gm_now + column(H1) * gm_lag
        if j == LEVELS - 1:
            level_sums[0] = low0 * gm_now + low1 * gm_lag
    scale = float(NZ * SPAN) ** (-0.5)
    every = [s * (R * scale) for s in low_sums + high_sums] + [s * scale for s in level_sums]
    lane = lax.broadcasted_iota(jnp.int32, (ROWS, BLOCK), 1) - group * len(every)
    found = jnp.zeros((ROWS, BLOCK), F32)
    for k, value in enumerate(every):
        found = jnp.where(lane == k, jnp.sum(value, 1, keepdims=True), found)

    @pl.when(group == 0)
    def _():
        small[...] = found

    @pl.when(group > 0)
    def _():
        small[...] = small[...] + found

    @pl.when(group == 64 // ROWS - 1)
    def _():
        for block in range(8):
            out_ref[block, 64:] = small[...].astype(BF16)


def backward(own, halo, inputs, levels, coef):
    rows = pl.BlockSpec((8, ROWS, BLOCK), lambda g: (0, g, 0))
    return pl.pallas_call(
        backward_kernel,
        grid=(64 // ROWS,),
        in_specs=[
            rows,
            rows,
            rows,
            pl.BlockSpec((LEVELS - 1, 8, ROWS, BLOCK), lambda g: (0, 0, g, 0)),
            pl.BlockSpec((ROWS, 128), lambda g: (g, 0)),
        ],
        out_specs=pl.BlockSpec((8, 64 + ROWS, BLOCK), lambda g: (0, 0, 0)),
        out_shape=jax.ShapeDtypeStruct((8, 64 + ROWS, BLOCK), BF16),
        scratch_shapes=[
            pltpu.VMEM((ROWS, 2 * SPAN), F32),
            pltpu.VMEM((ROWS, 2 * SPAN), F32),
            pltpu.VMEM((ROWS, BLOCK), F32),
        ],
        compiler_params=PARAMS,
        cost_estimate=pl.CostEstimate(flops=40_000_000, bytes_accessed=4_000_000, transcendentals=0),
        name="backward_chain",
    )(own, halo, inputs, levels, coef)


def product_kernel(place_ref, *refs):
    z_refs, og_refs, out_ref, rows, total = refs[:4], refs[4:12], refs[12], refs[13], refs[14]
    y, x, core = place_ref[0], place_ref[1], place_ref[2]
    for k, steps in enumerate(ORDER):
        source = lax.rem(y + (NY - steps), NY)
        for block in range(8):
            rows[block, pl.ds(pl.multiple_of(source * 64, 64), 64), :] = z_refs[k][block]
    for k in range(8):
        steps, flip = ORDER[k // 2], k % 2
        block = lax.rem(x + (NX - steps), NX) * 2 + (core if flip == 0 else 1 - core)
        part = lax.dot_general(
            rows[block], og_refs[k][...], (((1,), (1,)), ((), ())), preferred_element_type=F32
        )
        total[...] = part if k == 0 else total[...] + part
    scale = float(NZ * SPAN) ** (-0.5)
    for chunk in range(8):
        out_ref[chunk, :32] = (total[chunk * 32 : (chunk + 1) * 32] * scale).astype(BF16)


def product(place, z_pieces, og_pieces):
    whole = pl.BlockSpec(memory_space=pltpu.VMEM)
    return pl.pallas_call(
        product_kernel,
        in_specs=[pl.BlockSpec(memory_space=pltpu.SMEM)] + [whole] * 12,
        out_specs=whole,
        out_shape=jax.ShapeDtypeStruct((8, 32 + ROWS, 512), BF16),
        scratch_shapes=[pltpu.VMEM((8, 256, BLOCK), BF16), pltpu.VMEM((256, 512), F32)],
        compiler_params=PARAMS,
        cost_estimate=pl.CostEstimate(flops=540_000_000, bytes_accessed=4_000_000, transcendentals=0),
        name="mix_product",
    )(place, *z_pieces, *og_pieces)


def partials_kernel(place_ref, mix_ref, og_ref, one_ref, three_ref, two_ref, own_ref):
    y = place_ref[0]
    for steps, ref in ((1, one_ref), (3, three_ref), (2, two_ref), (0, own_ref)):
        start = pl.multiple_of(lax.rem(y + steps, NY) * 512, 512)
        part = jnp.dot(mix_ref[pl.ds(start, 512), :], og_ref[...], preferred_element_type=F32)
        ref[...] = part.astype(ref.dtype)


def partials(place, mix, out_grad):
    whole = pl.BlockSpec(memory_space=pltpu.VMEM)
    return pl.pallas_call(
        partials_kernel,
        in_specs=[pl.BlockSpec(memory_space=pltpu.SMEM), whole, whole],
        out_specs=[whole] * 4,
        out_shape=[jax.ShapeDtypeStruct((512, BLOCK), BF16)] * 3 + [jax.ShapeDtypeStruct((512, BLOCK), F32)],
        compiler_params=PARAMS,
        cost_estimate=pl.CostEstimate(flops=1_080_000_000, bytes_accessed=3_500_000, transcendentals=0),
        name="grad_z_partials",
    )(place, mix, out_grad)


def spread_kernel(*refs):
    ins, out_ref = refs[:-1], refs[-1]
    for half in range(2):
        for block in range(8):
            rows = pl.ds(half * 256 + block * 32, 32)
            total = ins[0][rows, :]
            for ref in ins[1:]:
                total = total + ref[rows, :].astype(F32)
            out_ref[block, half * 32 : (half + 1) * 32] = total.astype(BF16)


def spread(*values):
    whole = pl.BlockSpec(memory_space=pltpu.VMEM)
    return pl.pallas_call(
        spread_kernel,
        in_specs=[whole] * len(values),
        out_specs=whole,
        out_shape=jax.ShapeDtypeStruct((8, 64, BLOCK), BF16),
        compiler_params=PARAMS,
        cost_estimate=pl.CostEstimate(flops=500_000, bytes_accessed=1_000_000, transcendentals=0),
        name="rows_by_device",
    )(*values)


def gather_kernel(in_ref, out_ref):
    for half in range(2):
        for block in range(8):
            rows = pl.ds(half * 256 + block * 32, 32)
            out_ref[rows, :] = in_ref[block, half * 32 : (half + 1) * 32]


def gathered(value):
    whole = pl.BlockSpec(memory_space=pltpu.VMEM)
    return pl.pallas_call(
        gather_kernel,
        in_specs=[whole],
        out_specs=whole,
        out_shape=jax.ShapeDtypeStruct((512, BLOCK), BF16),
        compiler_params=PARAMS,
        cost_estimate=pl.CostEstimate(flops=0, bytes_accessed=600_000, transcendentals=0),
        name="grad_inputs_rows",
    )(value)


def pack_kernel(part_ref, sums_ref, out_ref):
    pieces = []
    for pair in range(4):
        odd = pltpu.roll(sums_ref[2 * pair + 1].astype(F32), 64, 1)
        pieces.append((sums_ref[2 * pair].astype(F32) + odd).astype(BF16))
    packed = jnp.concatenate(pieces, 1)
    for plane in range(NZ):
        out_ref[plane] = packed


def packed(part, grad_in):
    return pl.pallas_call(
        pack_kernel,
        grid=(1,),
        in_specs=[
            pl.BlockSpec(memory_space=pl.ANY),
            pl.BlockSpec((8, ROWS, 128), lambda g: (0, 64 // ROWS, 0)),
        ],
        out_specs=pl.BlockSpec((NZ, ROWS, 512), lambda g: (0, 32 // ROWS, 0)),
        out_shape=jax.ShapeDtypeStruct((NZ, 32 + ROWS, 512), BF16),
        input_output_aliases={0: 0},
        compiler_params=PARAMS,
        cost_estimate=pl.CostEstimate(flops=20_000, bytes_accessed=200_000, transcendentals=0),
        name="pack_sums",
    )(part, grad_in)


def sums_kernel(in_ref, mix_ref, low_ref, high_ref, level_ref):
    total = in_ref[0].astype(F32)
    for plane in range(1, NZ):
        total = total + in_ref[plane].astype(F32)
    mix_ref[...] = total[:32]
    for pair in range(4):
        turned = total[32:, pair * 128 : (pair + 1) * 128].T
        for odd in range(2):
            for group in range(64 // ROWS):
                at = (group // 2) * 256 + (2 * pair + odd) * 32 + (group % 2) * ROWS
                part = turned[odd * 64 + group * 16 : odd * 64 + (group + 1) * 16]
                low_ref[:, at : at + ROWS] = part[:2]
                high_ref[:, at : at + ROWS] = part[2:4]
                level_ref[:, at : at + ROWS] = part[4:]


def plane_sums(value):
    whole = pl.BlockSpec(memory_space=pltpu.VMEM)
    return pl.pallas_call(
        sums_kernel,
        in_specs=[whole],
        out_specs=[whole] * 4,
        out_shape=[jax.ShapeDtypeStruct((rows, 512), F32) for rows in (32, 2, 2, 12)],
        compiler_params=PARAMS,
        cost_estimate=pl.CostEstimate(flops=200_000, bytes_accessed=450_000, transcendentals=0),
        name="plane_sums",
    )(value)


def exchanged(value, axes):
    return lax.all_to_all(value, axes, 0, 0, tiled=True)


def after(value, *others):
    return lax.optimization_barrier((value, *others))[0]


def shards(inputs, out_grad, low_pass, high_pass, level_weight, mix):
    y, x, core = lax.axis_index("y"), lax.axis_index("x"), lax.axis_index("core")
    mine = x * NC + core
    place = jnp.stack([y, x, core]).astype(jnp.int32)

    one, three, two, grad_z = partials(place, mix, out_grad)
    arrived = [shift(value, "y", steps) for value, steps in ((one, 1), (three, 3), (two, 2))]

    own = exchanged(spread(after(inputs, grad_z)), PLANE)
    halo = shift(own, "z", 1, wrap=False)
    grad_z = exchanged(spread(grad_z, *arrived), PLANE)

    og_x = [out_grad] + [shift(out_grad, "x", steps) for steps in (1, 3)]
    og_x += [shift(after(out_grad, own), "x", 2)]

    own_rows = [low_pass * R, level_weight[1:] * (R * high_pass[0]), level_weight[1:] * (R * high_pass[1])]
    own_rows += [level_weight[:1], R * high_pass, level_weight[1:]]
    table = jnp.concatenate(own_rows, 0)
    table = lax.dynamic_slice_in_dim(table.reshape(-1, 2, 8, 32), mine, 1, 2).reshape(-1, 64)
    coef = jnp.pad(table, ((0, 128 - table.shape[0]), (0, 0))).T

    z, slope, levels = forward(own, halo, coef)
    z_all = [z] + [shift(z, "y", steps) for steps in (1, 3, 2)]

    grad_mixed = (grad_z.astype(F32) * slope).astype(BF16)
    grad_halo = shift(grad_mixed, "z", -1, wrap=False)
    grad_in = backward(grad_mixed, grad_halo, own, levels, coef)
    og = []
    for piece in og_x:
        og += [piece, shift(after(piece, grad_in), "core", 1)]
    grad_in = exchanged(grad_in, PLANE)
    part = product(place, z_all, og)
    grad_mix, low, high, level = plane_sums(exchanged(packed(part, grad_in), "z"))
    return gathered(grad_in), low, high, level, grad_mix


def solution(mesh):
    mesh = Mesh(mesh.devices.reshape(NZ, NX, NC, NY), ("z", "x", "core", "y"))
    wide, tall = P("y", CTX), P(None, "y")
    return jax.shard_map(
        shards,
        mesh=mesh,
        in_specs=(wide, wide, tall, tall, tall, tall),
        out_specs=(wide, tall, tall, tall, P(CTX, "y")),
        check_vma=False,
    )
```

time: 539 us -> 99.1 us (0.18)
  the two profiles are of different devices: /device:TPU:152 before, /device:TPU:8 now
where the time goes in v1:
time: 99.1 us; the launch traced here: 98.4 us
  starting transfers between devices  41 us (41%)
  waiting for transfers between devices  28.5 us (29%)
  Pallas kernels  19.7 us (20%)
  local copies, waits for them, and re-layouts  7.2 us (7%)
  other arithmetic  1.11 us (1%)
    all_to_all x4, starting transfers between devices, exchanged(): return lax.all_to_all(value, axes, 0, 0, tiled=True)  21.9 us
    all_to_all x4, waiting for transfers between devices, exchanged(): return lax.all_to_all(value, axes, 0, 0, tiled=True)  21.1 us
    ppermute x15, starting transfers between devices, shift(): return lax.ppermute(value, axis, pairs)  19.2 us
    ppermute x15, waiting for transfers between devices, shift(): return lax.ppermute(value, axis, pairs)  7.4 us
    unnamed x22, local copies, waits for them, and re-layouts  6.56 us
    pallas_call x1, Pallas kernels, backward(): pl.pallas_call(backward_kernel, grid=(64 // ROWS,), in_specs=[rows, rows,...  6.32 us
    pallas_call x1, Pallas kernels, forward(): pl.pallas_call(forward_kernel, grid=(64 // ROWS,), in_specs=[rows, rows,...  5.09 us
    pallas_call x1, Pallas kernels, product(): pl.pallas_call(product_kernel, in_specs=[pl.BlockSpec(memory_space=pltpu....  2.64 us
  transfers between devices with their start and end apart: 19, of which 7 were waited for; matrix products, arithmetic and copies ran while one was open for 1% of the time, Pallas kernels for 16%

profile of v1, /device:TPU:8, one launch (start us, length us, event | category | flops | bytes accessed | tf_op | source)
XLA Modules:
  0.0 98.4 jit_solution(1706676650415633834)
XLA Ops:
  0.6 0.1 pad_add_fusion.place_ref
  0.7 1.6 %copy-done.7 = bf16[2048,512]{1,0:T(8,128)(2,1)S(1)} copy-done((bf16[2048,512]{1,0:T(8,128)(2,1)S(1)}, bf16[2048,512]{1,0:T(8,128)(2,1)}, u32[]{:S(2)}) %copy-start.7) | copy-done | bytes 2097176
  2.3 1.7 %grad_z_partials.1 = (bf16[512,256]{1,0:T(8,128)(2,1)S(1)}, bf16[512,256]{1,0:T(8,128)(2,1)S(1)}, bf16[512,256]{1,0:T(8,128)(2,1)S(1)}, f32[512,256]{1,0:T(8,128)S(1)}) custom-call(s32[3]{0:T(128)S(1)} %pad_add_fusion.place_ref, bf16[2048,512]{1,0:T(8,128)(2,1)S(1)} %copy-done.7, bf16[512,256]{1,0:T(8,128)(2,1)} %refs_4_.1), custom_call_target="tpu_custom_call" | custom-call | flops 1080000000 | bytes 3500000 | tf_op jit(solution)/shard_map/grad_z_partials/pallas_call | solution.py:267
  4.1 0.7 rows_by_device.3
  4.8 4.3 %all-to-all-start.1 = ((bf16[8,64,256]{2,1,0:T(8,128)(2,1)}), bf16[8,64,256]{2,1,0:T(8,128)(2,1)S(1)}, u32[]{:S(2)}, u32[]{:S(2)}) async-start(bf16[8,64,256]{2,1,0:T(8,128)(2,1)} %rows_by_device.3), calls=%async_computation.1 | async-start | bytes 524288 | tf_op jit(solution)/shard_map/all_to_all | solution.py:379
  9.1 1.6 %collective-permute-start = (bf16[512,256]{1,0:T(8,128)(2,1)S(1)}, bf16[512,256]{1,0:T(8,128)(2,1)S(1)}, u32[]{:S(2)}, u32[]{:S(2)}) collective-permute-start(bf16[512,256]{1,0:T(8,128)(2,1)S(1)} %get-tuple-element.23), channel_id=1, source_target_pairs={{0,1},{1,2},{2,3},{3,0},{4,5},{5,6},{6,7},{7,4},{8,9},{9,10},{10,1... | collective-permute-start | bytes 786440 | tf_op jit(solution)/shard_map/ppermute | solution.py:27
  10.7 0.4 collective-permute-start.1
  11.1 2.3 %collective-permute-start.2 = (bf16[512,256]{1,0:T(8,128)(2,1)S(1)}, bf16[512,256]{1,0:T(8,128)(2,1)S(1)}, u32[]{:S(2)}, u32[]{:S(2)}) collective-permute-start(bf16[512,256]{1,0:T(8,128)(2,1)S(1)} %get-tuple-element.25), channel_id=1, source_target_pairs={{0,2},{1,3},{2,0},{3,1},{4,6},{5,7},{6,4},{7,5},{8,10},{9,11},{10,... | collective-permute-start | bytes 786440 | tf_op jit(solution)/shard_map/ppermute | solution.py:27
  13.4 3.2 %all-to-all-done.1.own_ref.inputs_ref = bf16[8,64,256]{2,1,0:T(8,128)(2,1)S(1)} async-done(((bf16[8,64,256]{2,1,0:T(8,128)(2,1)}), bf16[8,64,256]{2,1,0:T(8,128)(2,1)S(1)}, u32[]{:S(2)}, u32[]{:S(2)}) %all-to-all-start.1) | async-done | bytes 262176 | tf_op jit(solution)/shard_map/all_to_all | solution.py:379
  16.6 3.8 %collective-permute-start.3 = (bf16[8,64,256]{2,1,0:T(8,128)(2,1)S(1)}, bf16[8,64,256]{2,1,0:T(8,128)(2,1)S(1)}, u32[]{:S(2)}, u32[]{:S(2)}) collective-permute-start(bf16[8,64,256]{2,1,0:T(8,128)(2,1)S(1)} %all-to-all-done.1.own_ref.inputs_ref), channel_id=1, source_target_pairs={{0,32},{32,64},{64,96},{96,128},{128,160},{160,192},{192,224},{1,3... | collective-permute-start | bytes 786440 | tf_op jit(solution)/shard_map/ppermute | solution.py:27
  20.5 0.4 concatenate.3
  20.9 0.1 reshape.16
  21.0 4.4 %collective-permute-done.2.refs_3_ = bf16[512,256]{1,0:T(8,128)(2,1)S(1)} collective-permute-done((bf16[512,256]{1,0:T(8,128)(2,1)S(1)}, bf16[512,256]{1,0:T(8,128)(2,1)S(1)}, u32[]{:S(2)}, u32[]{:S(2)}) %collective-permute-start.2) | collective-permute-done | bytes 262176 | tf_op jit(solution)/shard_map/ppermute | solution.py:27
  25.4 0.8 rows_by_device.2
  26.2 4.4 %all-to-all-start = ((bf16[8,64,256]{2,1,0:T(8,128)(2,1)}), bf16[8,64,256]{2,1,0:T(8,128)(2,1)}, u32[]{:S(2)}, u32[]{:S(2)}) async-start(bf16[8,64,256]{2,1,0:T(8,128)(2,1)} %rows_by_device.2), calls=%async_computation | async-start | bytes 524288 | tf_op jit(solution)/shard_map/all_to_all | solution.py:379
  30.7 0.1 copy.13
  30.8 0.0 copy-start.1
  30.8 0.7 copy-done.1
  31.5 0.9 copy-done.2
  32.5 5.1 %forward_chain.1 = (bf16[8,64,256]{2,1,0:T(8,128)(2,1)}, f32[8,64,256]{2,1,0:T(8,128)S(1)}, bf16[10,8,64,256]{3,2,1,0:T(8,128)(2,1)S(1)}) custom-call(bf16[8,64,256]{2,1,0:T(8,128)(2,1)S(1)} %all-to-all-done.1.own_ref.inputs_ref, bf16[8,64,256]{2,1,0:T(8,128)(2,1)S(1)} %copy-done.2, f32[64,128]{1,0:T(8,128)S(1)} %pad_bitcast_fusion.coef_ref), custom_call_target="tpu_custom_call" | custom-call | flops 40000000 | bytes 4000000 | tf_op jit(solution)/shard_map/forward_chain/pallas_call | solution.py:93
  37.6 0.8 all-to-all-done
  38.3 1.0 %multiply_convert_fusion.own_ref = bf16[8,64,256]{2,1,0:T(8,128)(2,1)S(1)} fusion(f32[8,64,256]{2,1,0:T(8,128)S(1)} %get-tuple-element.27, bf16[8,64,256]{2,1,0:T(8,128)(2,1)} %all-to-all-done), kind=kLoop, calls=%fused_computation | loop fusion | flops 393216 | bytes 1048576 | tf_op jit(solution)/shard_map/convert_element_type | solution.py:410
  39.3 1.3 %collective-permute-start.4 = (bf16[8,64,256]{2,1,0:T(8,128)(2,1)S(1)}, bf16[8,64,256]{2,1,0:T(8,128)(2,1)S(1)}, u32[]{:S(2)}, u32[]{:S(2)}) collective-permute-start(bf16[8,64,256]{2,1,0:T(8,128)(2,1)S(1)} %multiply_convert_fusion.own_ref), channel_id=1, source_target_pairs={{32,0},{64,32},{96,64},{128,96},{160,128},{192,160},{224,192},{33,... | collective-permute-start | bytes 786440 | tf_op jit(solution)/shard_map/ppermute | solution.py:27
  40.6 2.9 %collective-permute-start.13 = (bf16[512,256]{1,0:T(8,128)(2,1)}, bf16[512,256]{1,0:T(8,128)(2,1)S(1)}, u32[]{:S(2)}, u32[]{:S(2)}) collective-permute-start(bf16[512,256]{1,0:T(8,128)(2,1)} %refs_4_.1), channel_id=1, source_target_pairs={{0,16},{8,24},{16,0},{24,8},{1,17},{9,25},{17,1},{25,9},{2,18},{10... | collective-permute-start | bytes 786440 | tf_op jit(solution)/shard_map/ppermute | solution.py:27
  43.5 1.2 %collective-permute-start.11 = (bf16[512,256]{1,0:T(8,128)(2,1)}, bf16[512,256]{1,0:T(8,128)(2,1)S(1)}, u32[]{:S(2)}, u32[]{:S(2)}) collective-permute-start(bf16[512,256]{1,0:T(8,128)(2,1)} %refs_4_.1), channel_id=1, source_target_pairs={{0,24},{8,0},{16,8},{24,16},{1,25},{9,1},{17,9},{25,17},{2,26},{10... | collective-permute-start | bytes 786440 | tf_op jit(solution)/shard_map/ppermute | solution.py:27
  44.7 0.9 collective-permute-start.9
  45.5 2.2 %collective-permute-start.7 = (bf16[8,64,256]{2,1,0:T(8,128)(2,1)}, bf16[8,64,256]{2,1,0:T(8,128)(2,1)S(1)}, u32[]{:S(2)}, u32[]{:S(2)}) collective-permute-start(bf16[8,64,256]{2,1,0:T(8,128)(2,1)} %get-tuple-element.29.refs_0_), channel_id=1, source_target_pairs={{0,2},{1,3},{2,0},{3,1},{4,6},{5,7},{6,4},{7,5},{8,10},{9,11},{10,... | collective-permute-start | bytes 786440 | tf_op jit(solution)/shard_map/ppermute | solution.py:27
  47.7 1.6 %collective-permute-done.4.halo_ref = bf16[8,64,256]{2,1,0:T(8,128)(2,1)S(1)} collective-permute-done((bf16[8,64,256]{2,1,0:T(8,128)(2,1)S(1)}, bf16[8,64,256]{2,1,0:T(8,128)(2,1)S(1)}, u32[]{:S(2)}, u32[]{:S(2)}) %collective-permute-start.4) | collective-permute-done | bytes 262176 | tf_op jit(solution)/shard_map/ppermute | solution.py:27
  49.4 0.9 collective-permute-start.6
  50.3 6.3 %backward_chain.1 = bf16[8,80,256]{2,1,0:T(8,128)(2,1)} custom-call(bf16[8,64,256]{2,1,0:T(8,128)(2,1)S(1)} %multiply_convert_fusion.own_ref, bf16[8,64,256]{2,1,0:T(8,128)(2,1)S(1)} %collective-permute-done.4.halo_ref, bf16[8,64,256]{2,1,0:T(8,128)(2,1)S(1)} %all-to-all-done.1.own_ref.inputs_ref, bf16[10,8,64,256]{3,2,1,0:T(8,128)(2,1)S(1)} %get-tuple-element.28.levels_ref, ...), custom_call_target="tpu_custom_call" | custom-call | flops 40000000 | bytes 4000000 | tf_op jit(solution)/shard_map/backward_chain/pallas_call | solution.py:201
  56.6 1.1 %collective-permute-start.5 = (bf16[8,64,256]{2,1,0:T(8,128)(2,1)}, bf16[8,64,256]{2,1,0:T(8,128)(2,1)S(1)}, u32[]{:S(2)}, u32[]{:S(2)}) collective-permute-start(bf16[8,64,256]{2,1,0:T(8,128)(2,1)} %get-tuple-element.29.refs_0_), channel_id=1, source_target_pairs={{0,1},{1,2},{2,3},{3,0},{4,5},{5,6},{6,7},{7,4},{8,9},{9,10},{10,1... | collective-permute-start | bytes 786440 | tf_op jit(solution)/shard_map/ppermute | solution.py:27
  57.7 0.0 collective-permute-start.8
  57.7 0.5 collective-permute-start.10
  58.3 0.7 copy-done.3
  58.9 0.1 collective-permute-start.12
  59.0 1.3 %collective-permute-done.6.refs_2_ = bf16[8,64,256]{2,1,0:T(8,128)(2,1)S(1)} collective-permute-done((bf16[8,64,256]{2,1,0:T(8,128)(2,1)}, bf16[8,64,256]{2,1,0:T(8,128)(2,1)S(1)}, u32[]{:S(2)}, u32[]{:S(2)}) %collective-permute-start.6) | collective-permute-done | bytes 262176 | tf_op jit(solution)/shard_map/ppermute | solution.py:27
  60.4 0.7 copy-done.5
  61.1 0.0 collective-permute-start.14
  61.1 3.8 %all-to-all-start.2 = ((bf16[8,80,256]{2,1,0:T(8,128)(2,1)}), bf16[8,80,256]{2,1,0:T(8,128)(2,1)S(1)}, u32[]{:S(2)}, u32[]{:S(2)}) async-start(bf16[8,80,256]{2,1,0:T(8,128)(2,1)} %backward_chain.1), calls=%async_computation.2 | async-start | bytes 655360 | tf_op jit(solution)/shard_map/all_to_all | solution.py:379
  64.9 0.9 copy-done.4
  65.9 0.9 copy-done.6
  66.8 2.6 %mix_product.1.part_ref = bf16[8,48,512]{2,1,0:T(8,128)(2,1)} custom-call(s32[3]{0:T(128)S(1)} %pad_add_fusion.place_ref, bf16[8,64,256]{2,1,0:T(8,128)(2,1)} %get-tuple-element.29.refs_0_, bf16[8,64,256]{2,1,0:T(8,128)(2,1)S(1)} %collective-permute-done.5.refs_1_, bf16[8,64,256]{2,1,0:T(8,128)(2,1)S(1)} %copy-done.6, bf16[8,64,256]{2,1,0:T(8,128)(2,1)S(1)} %copy-done.4, ...), custom_call_target="tpu_custom_call" | custom-call | flops 540000000 | bytes 4000000 | tf_op jit(solution)/shard_map/mix_product/pallas_call | solution.py:245
  69.5 3.7 %all-to-all-done.2.in_ref.sums_ref = bf16[8,80,256]{2,1,0:T(8,128)(2,1)S(1)} async-done(((bf16[8,80,256]{2,1,0:T(8,128)(2,1)}), bf16[8,80,256]{2,1,0:T(8,128)(2,1)S(1)}, u32[]{:S(2)}, u32[]{:S(2)}) %all-to-all-start.2) | async-done | bytes 327712 | tf_op jit(solution)/shard_map/all_to_all | solution.py:379
  73.1 0.8 pack_sums.1
  73.9 9.4 %all-to-all-start.3 = ((bf16[8,48,512]{2,1,0:T(8,128)(2,1)}), bf16[8,48,512]{2,1,0:T(8,128)(2,1)S(1)}, u32[]{:S(2)}, u32[]{:S(2)}) async-start(bf16[8,48,512]{2,1,0:T(8,128)(2,1)} %pack_sums.1), calls=%async_computation.3 | async-start | bytes 786432 | tf_op jit(solution)/shard_map/all_to_all | solution.py:379
  83.2 0.7 grad_inputs_rows.1
  84.0 13.5 %all-to-all-done.3.in_ref = bf16[8,48,512]{2,1,0:T(8,128)(2,1)S(1)} async-done(((bf16[8,48,512]{2,1,0:T(8,128)(2,1)}), bf16[8,48,512]{2,1,0:T(8,128)(2,1)S(1)}, u32[]{:S(2)}, u32[]{:S(2)}) %all-to-all-start.3) | async-done | bytes 393248 | tf_op jit(solution)/shard_map/all_to_all | solution.py:379
  97.5 0.9 plane_sums.1
  (33 shorter events, 0.1 us)
Async XLA Ops:
  0.6 3.4 %copy-start = (bf16[512,256]{1,0:T(8,128)(2,1)S(1)}, bf16[512,256]{1,0:T(8,128)(2,1)}, u32[]{:S(2)}) copy-start(bf16[512,256]{1,0:T(8,128)(2,1)} %refs_0_) | copy-start | bytes 786436
  0.7 1.6 %copy-start.7 = (bf16[2048,512]{1,0:T(8,128)(2,1)S(1)}, bf16[2048,512]{1,0:T(8,128)(2,1)}, u32[]{:S(2)}) copy-start(bf16[2048,512]{1,0:T(8,128)(2,1)} %mix_ref.1) | copy-start | bytes 6291460
  2.3 11.1 %copy-start.9 = (f32[2,512]{1,0:T(2,128)S(1)}, f32[2,512]{1,0:T(2,128)}, u32[]{:S(2)}) copy-start(f32[2,512]{1,0:T(2,128)} %param.9) | copy-start | bytes 12292
  2.3 11.1 %copy-start.8 = (f32[12,512]{1,0:T(8,128)S(1)}, f32[12,512]{1,0:T(8,128)}, u32[]{:S(2)}) copy-start(f32[12,512]{1,0:T(8,128)} %param.10) | copy-start | bytes 73732
  2.3 18.1 %copy-start.10 = (f32[2,512]{1,0:T(2,128)S(1)}, f32[2,512]{1,0:T(2,128)}, u32[]{:S(2)}) copy-start(f32[2,512]{1,0:T(2,128)} %param.8) | copy-start | bytes 12292
  2.3 18.2 %slice-start = ((f32[12,512]{1,0:T(8,128)}), f32[1,512]{1,0:T(1,128)S(1)}, s32[]{:S(2)}) async-start(f32[12,512]{1,0:T(8,128)} %param.10), calls=%async_computation.4 | async-start | bytes 4096 | tf_op jit(solution)/shard_map/slice | solution.py:402
  4.8 11.8 %all-to-all-start.1 = ((bf16[8,64,256]{2,1,0:T(8,128)(2,1)}), bf16[8,64,256]{2,1,0:T(8,128)(2,1)S(1)}, u32[]{:S(2)}, u32[]{:S(2)}) async-start(bf16[8,64,256]{2,1,0:T(8,128)(2,1)} %rows_by_device.3), calls=%async_computation.1 | async-start | bytes 524288 | tf_op jit(solution)/shard_map/all_to_all | solution.py:379
  9.1 11.9 %collective-permute-start = (bf16[512,256]{1,0:T(8,128)(2,1)S(1)}, bf16[512,256]{1,0:T(8,128)(2,1)S(1)}, u32[]{:S(2)}, u32[]{:S(2)}) collective-permute-start(bf16[512,256]{1,0:T(8,128)(2,1)S(1)} %get-tuple-element.23), channel_id=1, source_target_pairs={{0,1},{1,2},{2,3},{3,0},{4,5},{5,6},{6,7},{7,4},{8,9},{9,10},{10,1... | collective-permute-start | bytes 786440 | tf_op jit(solution)/shard_map/ppermute | solution.py:27
  10.7 10.4 %collective-permute-start.1 = (bf16[512,256]{1,0:T(8,128)(2,1)S(1)}, bf16[512,256]{1,0:T(8,128)(2,1)S(1)}, u32[]{:S(2)}, u32[]{:S(2)}) collective-permute-start(bf16[512,256]{1,0:T(8,128)(2,1)S(1)} %get-tuple-element.24), channel_id=1, source_target_pairs={{0,3},{1,0},{2,1},{3,2},{4,7},{5,4},{6,5},{7,6},{8,11},{9,8},{10,9... | collective-permute-start | bytes 786440 | tf_op jit(solution)/shard_map/ppermute | solution.py:27
  11.1 14.3 %collective-permute-start.2 = (bf16[512,256]{1,0:T(8,128)(2,1)S(1)}, bf16[512,256]{1,0:T(8,128)(2,1)S(1)}, u32[]{:S(2)}, u32[]{:S(2)}) collective-permute-start(bf16[512,256]{1,0:T(8,128)(2,1)S(1)} %get-tuple-element.25), channel_id=1, source_target_pairs={{0,2},{1,3},{2,0},{3,1},{4,6},{5,7},{6,4},{7,5},{8,10},{9,11},{10,... | collective-permute-start | bytes 786440 | tf_op jit(solution)/shard_map/ppermute | solution.py:27
  16.6 14.2 %collective-permute-start.3 = (bf16[8,64,256]{2,1,0:T(8,128)(2,1)S(1)}, bf16[8,64,256]{2,1,0:T(8,128)(2,1)S(1)}, u32[]{:S(2)}, u32[]{:S(2)}) collective-permute-start(bf16[8,64,256]{2,1,0:T(8,128)(2,1)S(1)} %all-to-all-done.1.own_ref.inputs_ref), channel_id=1, source_target_pairs={{0,32},{32,64},{64,96},{96,128},{128,160},{160,192},{192,224},{1,3... | collective-permute-start | bytes 786440 | tf_op jit(solution)/shard_map/ppermute | solution.py:27
  26.2 12.1 %all-to-all-start = ((bf16[8,64,256]{2,1,0:T(8,128)(2,1)}), bf16[8,64,256]{2,1,0:T(8,128)(2,1)}, u32[]{:S(2)}, u32[]{:S(2)}) async-start(bf16[8,64,256]{2,1,0:T(8,128)(2,1)} %rows_by_device.2), calls=%async_computation | async-start | bytes 524288 | tf_op jit(solution)/shard_map/all_to_all | solution.py:379
  30.8 0.7 copy-start.1
  31.5 0.9 copy-start.2
  39.3 10.0 %collective-permute-start.4 = (bf16[8,64,256]{2,1,0:T(8,128)(2,1)S(1)}, bf16[8,64,256]{2,1,0:T(8,128)(2,1)S(1)}, u32[]{:S(2)}, u32[]{:S(2)}) collective-permute-start(bf16[8,64,256]{2,1,0:T(8,128)(2,1)S(1)} %multiply_convert_fusion.own_ref), channel_id=1, source_target_pairs={{32,0},{64,32},{96,64},{128,96},{160,128},{192,160},{224,192},{33,... | collective-permute-start | bytes 786440 | tf_op jit(solution)/shard_map/ppermute | solution.py:27
  40.6 15.9 %collective-permute-start.13 = (bf16[512,256]{1,0:T(8,128)(2,1)}, bf16[512,256]{1,0:T(8,128)(2,1)S(1)}, u32[]{:S(2)}, u32[]{:S(2)}) collective-permute-start(bf16[512,256]{1,0:T(8,128)(2,1)} %refs_4_.1), channel_id=1, source_target_pairs={{0,16},{8,24},{16,0},{24,8},{1,17},{9,25},{17,1},{25,9},{2,18},{10... | collective-permute-start | bytes 786440 | tf_op jit(solution)/shard_map/ppermute | solution.py:27
  43.5 14.2 %collective-permute-start.11 = (bf16[512,256]{1,0:T(8,128)(2,1)}, bf16[512,256]{1,0:T(8,128)(2,1)S(1)}, u32[]{:S(2)}, u32[]{:S(2)}) collective-permute-start(bf16[512,256]{1,0:T(8,128)(2,1)} %refs_4_.1), channel_id=1, source_target_pairs={{0,24},{8,0},{16,8},{24,16},{1,25},{9,1},{17,9},{25,17},{2,26},{10... | collective-permute-start | bytes 786440 | tf_op jit(solution)/shard_map/ppermute | solution.py:27
  44.7 13.1 %collective-permute-start.9 = (bf16[512,256]{1,0:T(8,128)(2,1)}, bf16[512,256]{1,0:T(8,128)(2,1)}, u32[]{:S(2)}, u32[]{:S(2)}) collective-permute-start(bf16[512,256]{1,0:T(8,128)(2,1)} %refs_4_.1), channel_id=1, source_target_pairs={{0,8},{8,16},{16,24},{24,0},{1,9},{9,17},{17,25},{25,1},{2,10},{10... | collective-permute-start | bytes 786440 | tf_op jit(solution)/shard_map/ppermute | solution.py:27
  45.5 12.7 %collective-permute-start.7 = (bf16[8,64,256]{2,1,0:T(8,128)(2,1)}, bf16[8,64,256]{2,1,0:T(8,128)(2,1)S(1)}, u32[]{:S(2)}, u32[]{:S(2)}) collective-permute-start(bf16[8,64,256]{2,1,0:T(8,128)(2,1)} %get-tuple-element.29.refs_0_), channel_id=1, source_target_pairs={{0,2},{1,3},{2,0},{3,1},{4,6},{5,7},{6,4},{7,5},{8,10},{9,11},{10,... | collective-permute-start | bytes 786440 | tf_op jit(solution)/shard_map/ppermute | solution.py:27
  49.4 11.0 %collective-permute-start.6 = (bf16[8,64,256]{2,1,0:T(8,128)(2,1)}, bf16[8,64,256]{2,1,0:T(8,128)(2,1)S(1)}, u32[]{:S(2)}, u32[]{:S(2)}) collective-permute-start(bf16[8,64,256]{2,1,0:T(8,128)(2,1)} %get-tuple-element.29.refs_0_), channel_id=1, source_target_pairs={{0,3},{1,0},{2,1},{3,2},{4,7},{5,4},{6,5},{7,6},{8,11},{9,8},{10,9... | collective-permute-start | bytes 786440 | tf_op jit(solution)/shard_map/ppermute | solution.py:27
  56.6 8.3 %collective-permute-start.5 = (bf16[8,64,256]{2,1,0:T(8,128)(2,1)}, bf16[8,64,256]{2,1,0:T(8,128)(2,1)S(1)}, u32[]{:S(2)}, u32[]{:S(2)}) collective-permute-start(bf16[8,64,256]{2,1,0:T(8,128)(2,1)} %get-tuple-element.29.refs_0_), channel_id=1, source_target_pairs={{0,1},{1,2},{2,3},{3,0},{4,5},{5,6},{6,7},{7,4},{8,9},{9,10},{10,1... | collective-permute-start | bytes 786440 | tf_op jit(solution)/shard_map/ppermute | solution.py:27
  57.7 7.1 %collective-permute-start.8 = (bf16[512,256]{1,0:T(8,128)(2,1)}, bf16[512,256]{1,0:T(8,128)(2,1)S(1)}, u32[]{:S(2)}, u32[]{:S(2)}) collective-permute-start(bf16[512,256]{1,0:T(8,128)(2,1)} %refs_4_.1), channel_id=1, source_target_pairs={{0,4},{4,0},{1,5},{5,1},{2,6},{6,2},{3,7},{7,3},{8,12},{12,8},{9,1... | collective-permute-start | bytes 786440 | tf_op jit(solution)/shard_map/ppermute | solution.py:27
  57.7 7.1 %collective-permute-start.10 = (bf16[512,256]{1,0:T(8,128)(2,1)}, bf16[512,256]{1,0:T(8,128)(2,1)S(1)}, u32[]{:S(2)}, u32[]{:S(2)}) collective-permute-start(bf16[512,256]{1,0:T(8,128)(2,1)} %collective-permute-done.9.refs_6_), channel_id=1, source_target_pairs={{0,4},{4,0},{1,5},{5,1},{2,6},{6,2},{3,7},{7,3},{8,12},{12,8},{9,1... | collective-permute-start | bytes 786440 | tf_op jit(solution)/shard_map/ppermute | solution.py:27
  58.2 0.7 copy-start.3
  58.9 6.0 %collective-permute-start.12 = (bf16[512,256]{1,0:T(8,128)(2,1)S(1)}, bf16[512,256]{1,0:T(8,128)(2,1)S(1)}, u32[]{:S(2)}, u32[]{:S(2)}) collective-permute-start(bf16[512,256]{1,0:T(8,128)(2,1)S(1)} %collective-permute-done.11.refs_8_), channel_id=1, source_target_pairs={{0,4},{4,0},{1,5},{5,1},{2,6},{6,2},{3,7},{7,3},{8,12},{12,8},{9,1... | collective-permute-start | bytes 786440 | tf_op jit(solution)/shard_map/ppermute | solution.py:27
  60.4 0.7 copy-start.5
  61.1 3.8 %collective-permute-start.14 = (bf16[512,256]{1,0:T(8,128)(2,1)S(1)}, bf16[512,256]{1,0:T(8,128)(2,1)S(1)}, u32[]{:S(2)}, u32[]{:S(2)}) collective-permute-start(bf16[512,256]{1,0:T(8,128)(2,1)S(1)} %collective-permute-done.13.refs_10_), channel_id=1, source_target_pairs={{0,4},{4,0},{1,5},{5,1},{2,6},{6,2},{3,7},{7,3},{8,12},{12,8},{9,1... | collective-permute-start | bytes 786440 | tf_op jit(solution)/shard_map/ppermute | solution.py:27
  61.1 12.0 %all-to-all-start.2 = ((bf16[8,80,256]{2,1,0:T(8,128)(2,1)}), bf16[8,80,256]{2,1,0:T(8,128)(2,1)S(1)}, u32[]{:S(2)}, u32[]{:S(2)}) async-start(bf16[8,80,256]{2,1,0:T(8,128)(2,1)} %backward_chain.1), calls=%async_computation.2 | async-start | bytes 655360 | tf_op jit(solution)/shard_map/all_to_all | solution.py:379
  64.9 1.0 copy-start.4
  65.9 0.9 copy-start.6
  73.9 23.6 %all-to-all-start.3 = ((bf16[8,48,512]{2,1,0:T(8,128)(2,1)}), bf16[8,48,512]{2,1,0:T(8,128)(2,1)S(1)}, u32[]{:S(2)}, u32[]{:S(2)}) async-start(bf16[8,48,512]{2,1,0:T(8,128)(2,1)} %pack_sums.1), calls=%async_computation.3 | async-start | bytes 786432 | tf_op jit(solution)/shard_map/all_to_all | solution.py:379

commit v2 on v1

--- a/solution.py
+++ b/solution.py
@@ -27,11 +27,23 @@
     return lax.ppermute(value, axis, pairs)
 
 
-def forward_kernel(own_ref, halo_ref, coef_ref, z_ref, slope_ref, levels_ref, level, mixed):
+def forward_kernel(own_ref, halo_any, coef_ref, z_ref, slope_ref, levels_ref, level, mixed, halo_ref, sems):
+    group = pl.program_id(0)
+
+    def arriving(at):
+        rows = pl.ds(pl.multiple_of(at * ROWS, ROWS), ROWS)
+        return pltpu.make_async_copy(halo_any.at[:, rows, :], halo_ref.at[at], sems.at[at])
+
+    @pl.when(group == 0)
+    def _():
+        for at in range(64 // ROWS):
+            arriving(at).start()
+
     for block in range(8):
-        columns = pl.ds(block * BLOCK, BLOCK)
-        level[:, columns] = halo_ref[block].astype(F32)
         level[:, pl.ds(SPAN + block * BLOCK, BLOCK)] = own_ref[block].astype(F32)
+    arriving(group).wait()
+    for block in range(8):
+        level[:, pl.ds(block * BLOCK, BLOCK)] = halo_ref[group, block].astype(F32)
 
     def column(index):
         return coef_ref[:, index : index + 1]
@@ -88,23 +100,32 @@
                 level[:, pl.ds(start, STEP)] = after
 
 
+def in_hbm(value):
+    return pltpu.with_memory_space_constraint(value, pltpu.HBM)
+
+
 def forward(own, halo, coef):
     rows = pl.BlockSpec((8, ROWS, BLOCK), lambda g: (0, g, 0))
     return pl.pallas_call(
         forward_kernel,
         grid=(64 // ROWS,),
-        in_specs=[rows, rows, pl.BlockSpec((ROWS, 128), lambda g: (g, 0))],
+        in_specs=[rows, pl.BlockSpec(memory_space=pl.ANY), pl.BlockSpec((ROWS, 128), lambda g: (g, 0))],
         out_specs=[rows, rows, pl.BlockSpec((LEVELS - 1, 8, ROWS, BLOCK), lambda g: (0, 0, g, 0))],
         out_shape=[
-            jax.ShapeDtypeStruct((8, 64, BLOCK), BF16),
+            pltpu.HBM((8, 64, BLOCK), BF16),
             jax.ShapeDtypeStruct((8, 64, BLOCK), F32),
             jax.ShapeDtypeStruct((LEVELS - 1, 8, 64, BLOCK), BF16),
         ],
-        scratch_shapes=[pltpu.VMEM((ROWS, 2 * SPAN), F32), pltpu.VMEM((ROWS, SPAN), F32)],
+        scratch_shapes=[
+            pltpu.VMEM((ROWS, 2 * SPAN), F32),
+            pltpu.VMEM((ROWS, SPAN), F32),
+            pltpu.VMEM((64 // ROWS, 8, ROWS, BLOCK), BF16),
+            pltpu.SemaphoreType.DMA((64 // ROWS,)),
+        ],
         compiler_params=PARAMS,
         cost_estimate=pl.CostEstimate(flops=40_000_000, bytes_accessed=4_000_000, transcendentals=131072),
         name="forward_chain",
-    )(own, halo, coef)
+    )(own, in_hbm(halo), coef)
 
 
 def backward_kernel(own_ref, halo_ref, inputs_ref, levels_ref, coef_ref, out_ref, grad, mixed, small):
@@ -222,36 +243,49 @@
 
 
 def product_kernel(place_ref, *refs):
-    z_refs, og_refs, out_ref, rows, total = refs[:4], refs[4:12], refs[12], refs[13], refs[14]
+    z_refs, og_refs, out_ref = refs[:4], refs[4:12], refs[12]
+    rows, out_grads, total, z_sem, og_sem = refs[13:]
     y, x, core = place_ref[0], place_ref[1], place_ref[2]
+    copies = []
     for k, steps in enumerate(ORDER):
-        source = lax.rem(y + (NY - steps), NY)
-        for block in range(8):
-            rows[block, pl.ds(pl.multiple_of(source * 64, 64), 64), :] = z_refs[k][block]
+        source = pl.multiple_of(lax.rem(y + (NY - steps), NY) * 64, 64)
+        copies.append(pltpu.make_async_copy(z_refs[k], rows.at[:, pl.ds(source, 64), :], z_sem.at[k]))
     for k in range(8):
         steps, flip = ORDER[k // 2], k % 2
         block = lax.rem(x + (NX - steps), NX) * 2 + (core if flip == 0 else 1 - core)
+        copies.append(pltpu.make_async_copy(og_refs[k], out_grads.at[block], og_sem.at[k]))
+    for copy in copies:
+        copy.start()
+    for copy in copies:
+        copy.wait()
+    for block in range(8):
         part = lax.dot_general(
-            rows[block], og_refs[k][...], (((1,), (1,)), ((), ())), preferred_element_type=F32
+            rows[block], out_grads[block], (((1,), (1,)), ((), ())), preferred_element_type=F32
         )
-        total[...] = part if k == 0 else total[...] + part
+        total[...] = part if block == 0 else total[...] + part
     scale = float(NZ * SPAN) ** (-0.5)
     for chunk in range(8):
         out_ref[chunk, :32] = (total[chunk * 32 : (chunk + 1) * 32] * scale).astype(BF16)
 
 
 def product(place, z_pieces, og_pieces):
-    whole = pl.BlockSpec(memory_space=pltpu.VMEM)
+    anywhere = pl.BlockSpec(memory_space=pl.ANY)
     return pl.pallas_call(
         product_kernel,
-        in_specs=[pl.BlockSpec(memory_space=pltpu.SMEM)] + [whole] * 12,
-        out_specs=whole,
+        in_specs=[pl.BlockSpec(memory_space=pltpu.SMEM)] + [anywhere] * 12,
+        out_specs=pl.BlockSpec(memory_space=pltpu.VMEM),
         out_shape=jax.ShapeDtypeStruct((8, 32 + ROWS, 512), BF16),
-        scratch_shapes=[pltpu.VMEM((8, 256, BLOCK), BF16), pltpu.VMEM((256, 512), F32)],
+        scratch_shapes=[
+            pltpu.VMEM((8, 256, BLOCK), BF16),
+            pltpu.VMEM((8, 512, BLOCK), BF16),
+            pltpu.VMEM((256, 512), F32),
+            pltpu.SemaphoreType.DMA((4,)),
+            pltpu.SemaphoreType.DMA((8,)),
+        ],
         compiler_params=PARAMS,
         cost_estimate=pl.CostEstimate(flops=540_000_000, bytes_accessed=4_000_000, transcendentals=0),
         name="mix_product",
-    )(place, *z_pieces, *og_pieces)
+    )(place, *map(in_hbm, z_pieces), *map(in_hbm, og_pieces))
 
 
 def partials_kernel(place_ref, mix_ref, og_ref, one_ref, three_ref, two_ref, own_ref):
@@ -395,8 +429,10 @@
     halo = shift(own, "z", 1, wrap=False)
     grad_z = exchanged(spread(grad_z, *arrived), PLANE)
 
-    og_x = [out_grad] + [shift(out_grad, "x", steps) for steps in (1, 3)]
-    og_x += [shift(after(out_grad, own), "x", 2)]
+    near = [shift(out_grad, "x", steps) for steps in (1, 3)]
+    far = shift(after(out_grad, arrived[0]), "x", 2)
+    early = [out_grad, shift(after(out_grad, own), "core", 1), far, shift(far, "core", 1)]
+    grad_z, *early = lax.optimization_barrier((grad_z, *early))
 
     own_rows = [low_pass * R, level_weight[1:] * (R * high_pass[0]), level_weight[1:] * (R * high_pass[1])]
     own_rows += [level_weight[:1], R * high_pass, level_weight[1:]]
@@ -410,9 +446,10 @@
     grad_mixed = (grad_z.astype(F32) * slope).astype(BF16)
     grad_halo = shift(grad_mixed, "z", -1, wrap=False)
     grad_in = backward(grad_mixed, grad_halo, own, levels, coef)
-    og = []
-    for piece in og_x:
+    og = early[:2]
+    for piece in near:
         og += [piece, shift(after(piece, grad_in), "core", 1)]
+    og += early[2:]
     grad_in = exchanged(grad_in, PLANE)
     part = product(place, z_all, og)
     grad_mix, low, high, level = plane_sums(exchanged(packed(part, grad_in), "z"))

time: 99.1 us -> 95.8 us (0.967)
  local copies, waits for them, and re-layouts: 7.2 us -> 3.6 us
  waiting for transfers between devices: 28.5 us -> 25.3 us
  Pallas kernels: 19.7 us -> 22 us
  starting transfers between devices: 41 us -> 42.3 us
    ppermute x15, waiting for transfers between devices: 7.4 us -> 3.13 us  [shift(): return lax.ppermute(value, axis, pairs)]
    unnamed x22 -> x18, local copies, waits for them, and re-layouts: 6.56 us -> 2.96 us
    ppermute x15, starting transfers between devices: 19.2 us -> 21.7 us  [shift(): return lax.ppermute(value, axis, pairs)]
    pallas_call x1, Pallas kernels: 2.64 us -> 3.97 us  [product(): pl.pallas_call(product_kernel, in_specs=[pl.BlockSpec(memory_space=pltpu....]
    all_to_all x4, starting transfers between devices: 21.9 us -> 20.6 us  [exchanged(): return lax.all_to_all(value, axes, 0, 0, tiled=True)]
    all_to_all x4, waiting for transfers between devices: 21.1 us -> 22.2 us  [exchanged(): return lax.all_to_all(value, axes, 0, 0, tiled=True)]
  transfers between devices with their start and end apart: 19 -> 19, of which waited for: 7 -> 6; matrix products, arithmetic and copies ran while one was open for 1% -> 1% of each run, Pallas kernels for 16% -> 20%
where the time goes in v2:
time: 95.8 us; the launch traced here: 95.2 us
  starting transfers between devices  42.3 us (44%)
  waiting for transfers between devices  25.3 us (26%)
  Pallas kernels  22 us (23%)
  local copies, waits for them, and re-layouts  3.6 us (4%)
  other arithmetic  1.13 us (1%)
    all_to_all x4, waiting for transfers between devices, exchanged(): return lax.all_to_all(value, axes, 0, 0, tiled=True)  22.2 us
    ppermute x15, starting transfers between devices, shift(): return lax.ppermute(value, axis, pairs)  21.7 us
    all_to_all x4, starting transfers between devices, exchanged(): return lax.all_to_all(value, axes, 0, 0, tiled=True)  20.6 us
    pallas_call x1, Pallas kernels, backward(): pl.pallas_call(backward_kernel, grid=(64 // ROWS,), in_specs=[rows, rows,...  6.34 us
    pallas_call x1, Pallas kernels, forward(): pl.pallas_call(forward_kernel, grid=(64 // ROWS,), in_specs=[rows, pl.Blo...  6 us
    pallas_call x1, Pallas kernels, product(): pl.pallas_call(product_kernel, in_specs=[pl.BlockSpec(memory_space=pltpu....  3.97 us
    ppermute x15, waiting for transfers between devices, shift(): return lax.ppermute(value, axis, pairs)  3.13 us
    unnamed x18, local copies, waits for them, and re-layouts  2.96 us
  transfers between devices with their start and end apart: 19, of which 6 were waited for; matrix products, arithmetic and copies ran while one was open for 1% of the time, Pallas kernels for 20%

profile of v2, /device:TPU:8, one launch (start us, length us, event | category | flops | bytes accessed | tf_op | source)
XLA Modules:
  0.0 95.2 jit_solution(16036540446061811844)
XLA Ops:
  0.6 0.1 pad_add_fusion.place_ref
  0.7 1.6 %copy-done.1 = bf16[2048,512]{1,0:T(8,128)(2,1)S(1)} copy-done((bf16[2048,512]{1,0:T(8,128)(2,1)S(1)}, bf16[2048,512]{1,0:T(8,128)(2,1)}, u32[]{:S(2)}) %copy-start.1) | copy-done | bytes 2097176
  2.3 1.7 %grad_z_partials.1 = (bf16[512,256]{1,0:T(8,128)(2,1)S(1)}, bf16[512,256]{1,0:T(8,128)(2,1)S(1)}, bf16[512,256]{1,0:T(8,128)(2,1)S(1)}, f32[512,256]{1,0:T(8,128)S(1)}) custom-call(s32[3]{0:T(128)S(1)} %pad_add_fusion.place_ref, bf16[2048,512]{1,0:T(8,128)(2,1)S(1)} %copy-done.1, bf16[512,256]{1,0:T(8,128)(2,1)} %refs_4_), custom_call_target="tpu_custom_call" | custom-call | flops 1080000000 | bytes 3500000 | tf_op jit(solution)/shard_map/grad_z_partials/pallas_call | solution.py:301
  4.0 1.7 %collective-permute-start = (bf16[512,256]{1,0:T(8,128)(2,1)S(1)}, bf16[512,256]{1,0:T(8,128)(2,1)S(1)}, u32[]{:S(2)}, u32[]{:S(2)}) collective-permute-start(bf16[512,256]{1,0:T(8,128)(2,1)S(1)} %get-tuple-element.27), channel_id=1, source_target_pairs={{0,1},{1,2},{2,3},{3,0},{4,5},{5,6},{6,7},{7,4},{8,9},{9,10},{10,1... | collective-permute-start | bytes 786440 | tf_op jit(solution)/shard_map/ppermute | solution.py:27
  5.7 0.7 collective-permute-start.1
  6.4 2.0 %collective-permute-start.2 = (bf16[512,256]{1,0:T(8,128)(2,1)S(1)}, bf16[512,256]{1,0:T(8,128)(2,1)S(1)}, u32[]{:S(2)}, u32[]{:S(2)}) collective-permute-start(bf16[512,256]{1,0:T(8,128)(2,1)S(1)} %get-tuple-element.29), channel_id=1, source_target_pairs={{0,2},{1,3},{2,0},{3,1},{4,6},{5,7},{6,4},{7,5},{8,10},{9,11},{10,... | collective-permute-start | bytes 786440 | tf_op jit(solution)/shard_map/ppermute | solution.py:27
  8.5 0.7 rows_by_device.3
  9.2 4.3 %all-to-all-start.1 = ((bf16[8,64,256]{2,1,0:T(8,128)(2,1)}), bf16[8,64,256]{2,1,0:T(8,128)(2,1)S(1)}, u32[]{:S(2)}, u32[]{:S(2)}) async-start(bf16[8,64,256]{2,1,0:T(8,128)(2,1)} %rows_by_device.3), calls=%async_computation.1 | async-start | bytes 524288 | tf_op jit(solution)/shard_map/all_to_all | solution.py:413
  13.5 0.0 collective-permute-done.refs_1_
  13.5 3.5 %collective-permute-start.4 = (bf16[512,256]{1,0:T(8,128)(2,1)}, bf16[512,256]{1,0:T(8,128)(2,1)}, u32[]{:S(2)}, u32[]{:S(2)}) collective-permute-start(bf16[512,256]{1,0:T(8,128)(2,1)} %refs_4_), channel_id=1, source_target_pairs={{0,16},{8,24},{16,0},{24,8},{1,17},{9,25},{17,1},{25,9},{2,18},{10... | collective-permute-start | bytes 786440 | tf_op jit(solution)/shard_map/ppermute | solution.py:27
  17.0 4.4 %all-to-all-done.1.own_ref.inputs_ref = bf16[8,64,256]{2,1,0:T(8,128)(2,1)S(1)} async-done(((bf16[8,64,256]{2,1,0:T(8,128)(2,1)}), bf16[8,64,256]{2,1,0:T(8,128)(2,1)S(1)}, u32[]{:S(2)}, u32[]{:S(2)}) %all-to-all-start.1) | async-done | bytes 262176 | tf_op jit(solution)/shard_map/all_to_all | solution.py:413
  21.5 4.5 %collective-permute-start.6 = (bf16[8,64,256]{2,1,0:T(8,128)(2,1)S(1)}, bf16[8,64,256]{2,1,0:T(8,128)(2,1)}, u32[]{:S(2)}, u32[]{:S(2)}) collective-permute-start(bf16[8,64,256]{2,1,0:T(8,128)(2,1)S(1)} %all-to-all-done.1.own_ref.inputs_ref), channel_id=1, source_target_pairs={{0,32},{32,64},{64,96},{96,128},{128,160},{160,192},{192,224},{1,3... | collective-permute-start | bytes 786440 | tf_op jit(solution)/shard_map/ppermute | solution.py:27
  26.0 0.7 collective-permute-done.4.refs_10_
  26.7 0.0 collective-permute-start.5
  26.8 0.4 concatenate.3
  27.2 0.1 reshape.16
  27.3 0.0 collective-permute-done.1.refs_2_
  27.3 0.0 collective-permute-done.2.refs_3_
  27.3 0.8 rows_by_device.2
  28.2 4.0 %all-to-all-start = ((bf16[8,64,256]{2,1,0:T(8,128)(2,1)}), bf16[8,64,256]{2,1,0:T(8,128)(2,1)}, u32[]{:S(2)}, u32[]{:S(2)}) async-start(bf16[8,64,256]{2,1,0:T(8,128)(2,1)} %rows_by_device.2), calls=%async_computation | async-start | bytes 524288 | tf_op jit(solution)/shard_map/all_to_all | solution.py:413
  32.2 0.1 copy.13
  32.3 0.0 collective-permute-done.6.halo_any
  32.3 6.0 %forward_chain.1 = (bf16[8,64,256]{2,1,0:T(8,128)(2,1)}, f32[8,64,256]{2,1,0:T(8,128)S(1)}, bf16[10,8,64,256]{3,2,1,0:T(8,128)(2,1)S(1)}) custom-call(bf16[8,64,256]{2,1,0:T(8,128)(2,1)S(1)} %all-to-all-done.1.own_ref.inputs_ref, bf16[8,64,256]{2,1,0:T(8,128)(2,1)} %collective-permute-done.6.halo_any, f32[64,128]{1,0:T(8,128)S(1)} %pad_bitcast_fusion.coef_ref), custom_call_target="tpu_custom_call" | custom-call | flops 40000000 | bytes 4000000 | tf_op jit(solution)/shard_map/forward_chain/pallas_call | solution.py:109
  38.4 1.4 %all-to-all-done = bf16[8,64,256]{2,1,0:T(8,128)(2,1)} async-done(((bf16[8,64,256]{2,1,0:T(8,128)(2,1)}), bf16[8,64,256]{2,1,0:T(8,128)(2,1)}, u32[]{:S(2)}, u32[]{:S(2)}) %all-to-all-start) | async-done | bytes 262176 | tf_op jit(solution)/shard_map/all_to_all | solution.py:413
  39.7 0.0 collective-permute-done.3.refs_5_
  39.7 0.0 collective-permute-done.5.refs_11_
  39.7 1.0 %multiply_convert_fusion.own_ref = bf16[8,64,256]{2,1,0:T(8,128)(2,1)S(1)} fusion(f32[8,64,256]{2,1,0:T(8,128)S(1)} %get-tuple-element.34, bf16[8,64,256]{2,1,0:T(8,128)(2,1)} %all-to-all-done), kind=kLoop, calls=%fused_computation | loop fusion | flops 393216 | bytes 1048576 | tf_op jit(solution)/shard_map/convert_element_type | solution.py:446
  40.8 1.3 %collective-permute-start.7 = (bf16[8,64,256]{2,1,0:T(8,128)(2,1)S(1)}, bf16[8,64,256]{2,1,0:T(8,128)(2,1)S(1)}, u32[]{:S(2)}, u32[]{:S(2)}) collective-permute-start(bf16[8,64,256]{2,1,0:T(8,128)(2,1)S(1)} %multiply_convert_fusion.own_ref), channel_id=1, source_target_pairs={{32,0},{64,32},{96,64},{128,96},{160,128},{192,160},{224,192},{33,... | collective-permute-start | bytes 786440 | tf_op jit(solution)/shard_map/ppermute | solution.py:27
  42.1 0.7 collective-permute-start.11
  42.7 2.7 %collective-permute-start.13 = (bf16[512,256]{1,0:T(8,128)(2,1)}, bf16[512,256]{1,0:T(8,128)(2,1)S(1)}, u32[]{:S(2)}, u32[]{:S(2)}) collective-permute-start(bf16[512,256]{1,0:T(8,128)(2,1)} %refs_4_), channel_id=1, source_target_pairs={{0,24},{8,0},{16,8},{24,16},{1,25},{9,1},{17,9},{25,17},{2,26},{10... | collective-permute-start | bytes 786440 | tf_op jit(solution)/shard_map/ppermute | solution.py:27
  45.4 1.2 %collective-permute-start.10 = (bf16[8,64,256]{2,1,0:T(8,128)(2,1)}, bf16[8,64,256]{2,1,0:T(8,128)(2,1)}, u32[]{:S(2)}, u32[]{:S(2)}) collective-permute-start(bf16[8,64,256]{2,1,0:T(8,128)(2,1)} %get-tuple-element.36.refs_0_), channel_id=1, source_target_pairs={{0,2},{1,3},{2,0},{3,1},{4,6},{5,7},{6,4},{7,5},{8,10},{9,11},{10,... | collective-permute-start | bytes 786440 | tf_op jit(solution)/shard_map/ppermute | solution.py:27
  46.6 1.6 %collective-permute-start.8 = (bf16[8,64,256]{2,1,0:T(8,128)(2,1)}, bf16[8,64,256]{2,1,0:T(8,128)(2,1)}, u32[]{:S(2)}, u32[]{:S(2)}) collective-permute-start(bf16[8,64,256]{2,1,0:T(8,128)(2,1)} %get-tuple-element.36.refs_0_), channel_id=1, source_target_pairs={{0,1},{1,2},{2,3},{3,0},{4,5},{5,6},{6,7},{7,4},{8,9},{9,10},{10,1... | collective-permute-start | bytes 786440 | tf_op jit(solution)/shard_map/ppermute | solution.py:27
  48.2 2.3 %collective-permute-done.7.halo_ref = bf16[8,64,256]{2,1,0:T(8,128)(2,1)S(1)} collective-permute-done((bf16[8,64,256]{2,1,0:T(8,128)(2,1)S(1)}, bf16[8,64,256]{2,1,0:T(8,128)(2,1)S(1)}, u32[]{:S(2)}, u32[]{:S(2)}) %collective-permute-start.7) | collective-permute-done | bytes 262176 | tf_op jit(solution)/shard_map/ppermute | solution.py:27
  50.5 1.3 %collective-permute-start.9 = (bf16[8,64,256]{2,1,0:T(8,128)(2,1)}, bf16[8,64,256]{2,1,0:T(8,128)(2,1)}, u32[]{:S(2)}, u32[]{:S(2)}) collective-permute-start(bf16[8,64,256]{2,1,0:T(8,128)(2,1)} %get-tuple-element.36.refs_0_), channel_id=1, source_target_pairs={{0,3},{1,0},{2,1},{3,2},{4,7},{5,4},{6,5},{7,6},{8,11},{9,8},{10,9... | collective-permute-start | bytes 786440 | tf_op jit(solution)/shard_map/ppermute | solution.py:27
  51.9 6.3 %backward_chain.1 = bf16[8,80,256]{2,1,0:T(8,128)(2,1)} custom-call(bf16[8,64,256]{2,1,0:T(8,128)(2,1)S(1)} %multiply_convert_fusion.own_ref, bf16[8,64,256]{2,1,0:T(8,128)(2,1)S(1)} %collective-permute-done.7.halo_ref, bf16[8,64,256]{2,1,0:T(8,128)(2,1)S(1)} %all-to-all-done.1.own_ref.inputs_ref, bf16[10,8,64,256]{3,2,1,0:T(8,128)(2,1)S(1)} %get-tuple-element.35.levels_ref, ...), custom_call_target="tpu_custom_call" | custom-call | flops 40000000 | bytes 4000000 | tf_op jit(solution)/shard_map/backward_chain/pallas_call | solution.py:222
  58.2 0.0 collective-permute-start.12
  58.2 0.0 collective-permute-done.13.refs_8_
  58.3 0.5 collective-permute-start.14
  58.7 4.0 %all-to-all-start.2 = ((bf16[8,80,256]{2,1,0:T(8,128)(2,1)}), bf16[8,80,256]{2,1,0:T(8,128)(2,1)S(1)}, u32[]{:S(2)}, u32[]{:S(2)}) async-start(bf16[8,80,256]{2,1,0:T(8,128)(2,1)} %backward_chain.1), calls=%async_computation.2 | async-start | bytes 655360 | tf_op jit(solution)/shard_map/all_to_all | solution.py:413
  62.8 0.7 copy-done.4
  63.5 0.7 copy-done.5
  64.2 4.0 %mix_product.1.part_ref = bf16[8,48,512]{2,1,0:T(8,128)(2,1)} custom-call(s32[3]{0:T(128)S(1)} %pad_add_fusion.place_ref, bf16[8,64,256]{2,1,0:T(8,128)(2,1)} %get-tuple-element.36.refs_0_, bf16[8,64,256]{2,1,0:T(8,128)(2,1)} %collective-permute-done.8.refs_1_, bf16[8,64,256]{2,1,0:T(8,128)(2,1)} %collective-permute-done.9.refs_2_, ...), custom_call_target="tpu_custom_call" | custom-call | flops 540000000 | bytes 4000000 | tf_op jit(solution)/shard_map/mix_product/pallas_call | solution.py:273
  68.2 2.8 %all-to-all-done.2.in_ref.sums_ref = bf16[8,80,256]{2,1,0:T(8,128)(2,1)S(1)} async-done(((bf16[8,80,256]{2,1,0:T(8,128)(2,1)}), bf16[8,80,256]{2,1,0:T(8,128)(2,1)S(1)}, u32[]{:S(2)}, u32[]{:S(2)}) %all-to-all-start.2) | async-done | bytes 327712 | tf_op jit(solution)/shard_map/all_to_all | solution.py:413
  71.0 0.8 pack_sums.1
  71.8 8.3 %all-to-all-start.3 = ((bf16[8,48,512]{2,1,0:T(8,128)(2,1)}), bf16[8,48,512]{2,1,0:T(8,128)(2,1)S(1)}, u32[]{:S(2)}, u32[]{:S(2)}) async-start(bf16[8,48,512]{2,1,0:T(8,128)(2,1)} %pack_sums.1), calls=%async_computation.3 | async-start | bytes 786432 | tf_op jit(solution)/shard_map/all_to_all | solution.py:413
  80.0 0.7 grad_inputs_rows.1
  80.8 13.5 %all-to-all-done.3.in_ref = bf16[8,48,512]{2,1,0:T(8,128)(2,1)S(1)} async-done(((bf16[8,48,512]{2,1,0:T(8,128)(2,1)}), bf16[8,48,512]{2,1,0:T(8,128)(2,1)S(1)}, u32[]{:S(2)}, u32[]{:S(2)}) %all-to-all-start.3) | async-done | bytes 393248 | tf_op jit(solution)/shard_map/all_to_all | solution.py:413
  94.3 0.9 plane_sums.1
  (29 shorter events, 0.1 us)
Async XLA Ops:
  0.6 7.8 %copy-start = (bf16[512,256]{1,0:T(8,128)(2,1)S(1)}, bf16[512,256]{1,0:T(8,128)(2,1)}, u32[]{:S(2)}) copy-start(bf16[512,256]{1,0:T(8,128)(2,1)} %refs_0_) | copy-start | bytes 786436
  0.7 1.6 %copy-start.1 = (bf16[2048,512]{1,0:T(8,128)(2,1)S(1)}, bf16[2048,512]{1,0:T(8,128)(2,1)}, u32[]{:S(2)}) copy-start(bf16[2048,512]{1,0:T(8,128)(2,1)} %mix_ref.1) | copy-start | bytes 6291460
  2.3 14.7 %copy-start.7 = (f32[2,512]{1,0:T(2,128)S(1)}, f32[2,512]{1,0:T(2,128)}, u32[]{:S(2)}) copy-start(f32[2,512]{1,0:T(2,128)} %param.9) | copy-start | bytes 12292
  2.3 14.7 %copy-start.6 = (f32[12,512]{1,0:T(8,128)S(1)}, f32[12,512]{1,0:T(8,128)}, u32[]{:S(2)}) copy-start(f32[12,512]{1,0:T(8,128)} %param.10) | copy-start | bytes 73732
  2.3 24.4 %copy-start.8 = (f32[2,512]{1,0:T(2,128)S(1)}, f32[2,512]{1,0:T(2,128)}, u32[]{:S(2)}) copy-start(f32[2,512]{1,0:T(2,128)} %param.8) | copy-start | bytes 12292
  2.3 24.4 %slice-start = ((f32[12,512]{1,0:T(8,128)}), f32[1,512]{1,0:T(1,128)S(1)}, s32[]{:S(2)}) async-start(f32[12,512]{1,0:T(8,128)} %param.10), calls=%async_computation.4 | async-start | bytes 4096 | tf_op jit(solution)/shard_map/slice | solution.py:438
  4.0 9.5 %collective-permute-start = (bf16[512,256]{1,0:T(8,128)(2,1)S(1)}, bf16[512,256]{1,0:T(8,128)(2,1)S(1)}, u32[]{:S(2)}, u32[]{:S(2)}) collective-permute-start(bf16[512,256]{1,0:T(8,128)(2,1)S(1)} %get-tuple-element.27), channel_id=1, source_target_pairs={{0,1},{1,2},{2,3},{3,0},{4,5},{5,6},{6,7},{7,4},{8,9},{9,10},{10,1... | collective-permute-start | bytes 786440 | tf_op jit(solution)/shard_map/ppermute | solution.py:27
  5.7 21.6 %collective-permute-start.1 = (bf16[512,256]{1,0:T(8,128)(2,1)S(1)}, bf16[512,256]{1,0:T(8,128)(2,1)S(1)}, u32[]{:S(2)}, u32[]{:S(2)}) collective-permute-start(bf16[512,256]{1,0:T(8,128)(2,1)S(1)} %get-tuple-element.28), channel_id=1, source_target_pairs={{0,3},{1,0},{2,1},{3,2},{4,7},{5,4},{6,5},{7,6},{8,11},{9,8},{10,9... | collective-permute-start | bytes 786440 | tf_op jit(solution)/shard_map/ppermute | solution.py:27
  6.4 20.9 %collective-permute-start.2 = (bf16[512,256]{1,0:T(8,128)(2,1)S(1)}, bf16[512,256]{1,0:T(8,128)(2,1)S(1)}, u32[]{:S(2)}, u32[]{:S(2)}) collective-permute-start(bf16[512,256]{1,0:T(8,128)(2,1)S(1)} %get-tuple-element.29), channel_id=1, source_target_pairs={{0,2},{1,3},{2,0},{3,1},{4,6},{5,7},{6,4},{7,5},{8,10},{9,11},{10,... | collective-permute-start | bytes 786440 | tf_op jit(solution)/shard_map/ppermute | solution.py:27
  9.2 12.3 %all-to-all-start.1 = ((bf16[8,64,256]{2,1,0:T(8,128)(2,1)}), bf16[8,64,256]{2,1,0:T(8,128)(2,1)S(1)}, u32[]{:S(2)}, u32[]{:S(2)}) async-start(bf16[8,64,256]{2,1,0:T(8,128)(2,1)} %rows_by_device.3), calls=%async_computation.1 | async-start | bytes 524288 | tf_op jit(solution)/shard_map/all_to_all | solution.py:413
  13.5 13.2 %collective-permute-start.4 = (bf16[512,256]{1,0:T(8,128)(2,1)}, bf16[512,256]{1,0:T(8,128)(2,1)}, u32[]{:S(2)}, u32[]{:S(2)}) collective-permute-start(bf16[512,256]{1,0:T(8,128)(2,1)} %refs_4_), channel_id=1, source_target_pairs={{0,16},{8,24},{16,0},{24,8},{1,17},{9,25},{17,1},{25,9},{2,18},{10... | collective-permute-start | bytes 786440 | tf_op jit(solution)/shard_map/ppermute | solution.py:27
  21.5 18.3 %collective-permute-start.3 = (bf16[512,256]{1,0:T(8,128)(2,1)}, bf16[512,256]{1,0:T(8,128)(2,1)}, u32[]{:S(2)}, u32[]{:S(2)}) collective-permute-start(bf16[512,256]{1,0:T(8,128)(2,1)} %refs_4_), channel_id=1, source_target_pairs={{0,4},{4,0},{1,5},{5,1},{2,6},{6,2},{3,7},{7,3},{8,12},{12,8},{9,1... | collective-permute-start | bytes 786440 | tf_op jit(solution)/shard_map/ppermute | solution.py:27
  21.5 10.9 %collective-permute-start.6 = (bf16[8,64,256]{2,1,0:T(8,128)(2,1)S(1)}, bf16[8,64,256]{2,1,0:T(8,128)(2,1)}, u32[]{:S(2)}, u32[]{:S(2)}) collective-permute-start(bf16[8,64,256]{2,1,0:T(8,128)(2,1)S(1)} %all-to-all-done.1.own_ref.inputs_ref), channel_id=1, source_target_pairs={{0,32},{32,64},{64,96},{96,128},{128,160},{160,192},{192,224},{1,3... | collective-permute-start | bytes 786440 | tf_op jit(solution)/shard_map/ppermute | solution.py:27
  26.7 13.0 %collective-permute-start.5 = (bf16[512,256]{1,0:T(8,128)(2,1)}, bf16[512,256]{1,0:T(8,128)(2,1)}, u32[]{:S(2)}, u32[]{:S(2)}) collective-permute-start(bf16[512,256]{1,0:T(8,128)(2,1)} %collective-permute-done.4.refs_10_), channel_id=1, source_target_pairs={{0,4},{4,0},{1,5},{5,1},{2,6},{6,2},{3,7},{7,3},{8,12},{12,8},{9,1... | collective-permute-start | bytes 786440 | tf_op jit(solution)/shard_map/ppermute | solution.py:27
  28.2 11.6 %all-to-all-start = ((bf16[8,64,256]{2,1,0:T(8,128)(2,1)}), bf16[8,64,256]{2,1,0:T(8,128)(2,1)}, u32[]{:S(2)}, u32[]{:S(2)}) async-start(bf16[8,64,256]{2,1,0:T(8,128)(2,1)} %rows_by_device.2), calls=%async_computation | async-start | bytes 524288 | tf_op jit(solution)/shard_map/all_to_all | solution.py:413
  40.8 9.8 %collective-permute-start.7 = (bf16[8,64,256]{2,1,0:T(8,128)(2,1)S(1)}, bf16[8,64,256]{2,1,0:T(8,128)(2,1)S(1)}, u32[]{:S(2)}, u32[]{:S(2)}) collective-permute-start(bf16[8,64,256]{2,1,0:T(8,128)(2,1)S(1)} %multiply_convert_fusion.own_ref), channel_id=1, source_target_pairs={{32,0},{64,32},{96,64},{128,96},{160,128},{192,160},{224,192},{33,... | collective-permute-start | bytes 786440 | tf_op jit(solution)/shard_map/ppermute | solution.py:27
  42.1 16.2 %collective-permute-start.11 = (bf16[512,256]{1,0:T(8,128)(2,1)}, bf16[512,256]{1,0:T(8,128)(2,1)S(1)}, u32[]{:S(2)}, u32[]{:S(2)}) collective-permute-start(bf16[512,256]{1,0:T(8,128)(2,1)} %refs_4_), channel_id=1, source_target_pairs={{0,8},{8,16},{16,24},{24,0},{1,9},{9,17},{17,25},{25,1},{2,10},{10... | collective-permute-start | bytes 786440 | tf_op jit(solution)/shard_map/ppermute | solution.py:27
  42.7 15.5 %collective-permute-start.13 = (bf16[512,256]{1,0:T(8,128)(2,1)}, bf16[512,256]{1,0:T(8,128)(2,1)S(1)}, u32[]{:S(2)}, u32[]{:S(2)}) collective-permute-start(bf16[512,256]{1,0:T(8,128)(2,1)} %refs_4_), channel_id=1, source_target_pairs={{0,24},{8,0},{16,8},{24,16},{1,25},{9,1},{17,9},{25,17},{2,26},{10... | collective-permute-start | bytes 786440 | tf_op jit(solution)/shard_map/ppermute | solution.py:27
  45.4 17.4 %collective-permute-start.10 = (bf16[8,64,256]{2,1,0:T(8,128)(2,1)}, bf16[8,64,256]{2,1,0:T(8,128)(2,1)}, u32[]{:S(2)}, u32[]{:S(2)}) collective-permute-start(bf16[8,64,256]{2,1,0:T(8,128)(2,1)} %get-tuple-element.36.refs_0_), channel_id=1, source_target_pairs={{0,2},{1,3},{2,0},{3,1},{4,6},{5,7},{6,4},{7,5},{8,10},{9,11},{10,... | collective-permute-start | bytes 786440 | tf_op jit(solution)/shard_map/ppermute | solution.py:27
  46.6 16.1 %collective-permute-start.8 = (bf16[8,64,256]{2,1,0:T(8,128)(2,1)}, bf16[8,64,256]{2,1,0:T(8,128)(2,1)}, u32[]{:S(2)}, u32[]{:S(2)}) collective-permute-start(bf16[8,64,256]{2,1,0:T(8,128)(2,1)} %get-tuple-element.36.refs_0_), channel_id=1, source_target_pairs={{0,1},{1,2},{2,3},{3,0},{4,5},{5,6},{6,7},{7,4},{8,9},{9,10},{10,1... | collective-permute-start | bytes 786440 | tf_op jit(solution)/shard_map/ppermute | solution.py:27
  50.5 12.2 %collective-permute-start.9 = (bf16[8,64,256]{2,1,0:T(8,128)(2,1)}, bf16[8,64,256]{2,1,0:T(8,128)(2,1)}, u32[]{:S(2)}, u32[]{:S(2)}) collective-permute-start(bf16[8,64,256]{2,1,0:T(8,128)(2,1)} %get-tuple-element.36.refs_0_), channel_id=1, source_target_pairs={{0,3},{1,0},{2,1},{3,2},{4,7},{5,4},{6,5},{7,6},{8,11},{9,8},{10,9... | collective-permute-start | bytes 786440 | tf_op jit(solution)/shard_map/ppermute | solution.py:27
  58.2 4.6 %copy-start.2 = (bf16[512,256]{1,0:T(8,128)(2,1)}, bf16[512,256]{1,0:T(8,128)(2,1)S(1)}, u32[]{:S(2)}) copy-start(bf16[512,256]{1,0:T(8,128)(2,1)S(1)} %collective-permute-done.11.refs_6_) | copy-start | bytes 786436
  58.2 4.6 %collective-permute-start.12 = (bf16[512,256]{1,0:T(8,128)(2,1)S(1)}, bf16[512,256]{1,0:T(8,128)(2,1)S(1)}, u32[]{:S(2)}, u32[]{:S(2)}) collective-permute-start(bf16[512,256]{1,0:T(8,128)(2,1)S(1)} %collective-permute-done.11.refs_6_), channel_id=1, source_target_pairs={{0,4},{4,0},{1,5},{5,1},{2,6},{6,2},{3,7},{7,3},{8,12},{12,8},{9,1... | collective-permute-start | bytes 786440 | tf_op jit(solution)/shard_map/ppermute | solution.py:27
  58.2 4.6 %copy-start.3 = (bf16[512,256]{1,0:T(8,128)(2,1)}, bf16[512,256]{1,0:T(8,128)(2,1)S(1)}, u32[]{:S(2)}) copy-start(bf16[512,256]{1,0:T(8,128)(2,1)S(1)} %collective-permute-done.13.refs_8_) | copy-start | bytes 786436
  58.3 4.5 %collective-permute-start.14 = (bf16[512,256]{1,0:T(8,128)(2,1)S(1)}, bf16[512,256]{1,0:T(8,128)(2,1)S(1)}, u32[]{:S(2)}, u32[]{:S(2)}) collective-permute-start(bf16[512,256]{1,0:T(8,128)(2,1)S(1)} %collective-permute-done.13.refs_8_), channel_id=1, source_target_pairs={{0,4},{4,0},{1,5},{5,1},{2,6},{6,2},{3,7},{7,3},{8,12},{12,8},{9,1... | collective-permute-start | bytes 786440 | tf_op jit(solution)/shard_map/ppermute | solution.py:27
  58.7 12.2 %all-to-all-start.2 = ((bf16[8,80,256]{2,1,0:T(8,128)(2,1)}), bf16[8,80,256]{2,1,0:T(8,128)(2,1)S(1)}, u32[]{:S(2)}, u32[]{:S(2)}) async-start(bf16[8,80,256]{2,1,0:T(8,128)(2,1)} %backward_chain.1), calls=%async_computation.2 | async-start | bytes 655360 | tf_op jit(solution)/shard_map/all_to_all | solution.py:413
  62.8 0.7 copy-start.4
  63.5 0.7 copy-start.5
  71.8 22.5 %all-to-all-start.3 = ((bf16[8,48,512]{2,1,0:T(8,128)(2,1)}), bf16[8,48,512]{2,1,0:T(8,128)(2,1)S(1)}, u32[]{:S(2)}, u32[]{:S(2)}) async-start(bf16[8,48,512]{2,1,0:T(8,128)(2,1)} %pack_sums.1), calls=%async_computation.3 | async-start | bytes 786432 | tf_op jit(solution)/shard_map/all_to_all | solution.py:413
